TPU v7x, 32 devices: a whole 2x2x4 slice. The times are simulated.
32 devices in a mesh: seq: 8 (over z, x), batch: 4 (over y, core).
Axes of the slice: x: 2, y: 2, z: 4, core: 2. Of those that a mesh axis runs over, the one named last changes fastest.
Arguments:
- tokens: bfloat16 [8, 2048, 1024], P('batch', 'seq'), may hold values from -6 to 6
- cotangent: bfloat16 [8, 2048, 1024], P('batch', 'seq'), may hold values from -6 to 6
- lengths: int32 [8], P('batch'), may hold values from 128 to 2048, as said below
- span_order: int32 [8, 2], replicated, may hold values from 0 to 15, as said below
- attn_gain: bfloat16 [1024], P('seq'), may hold values from 0.5 to 1.5
- query_heads: bfloat16 [1024, 96], P('seq'), may hold values from -0.375 to 0.375
- query_dims: bfloat16 [1024, 384], P('seq'), may hold values from -0.375 to 0.375
- key_heads: bfloat16 [1024, 32], P('seq'), may hold values from -0.25 to 0.25
- key_dims: bfloat16 [1024, 128], P('seq'), may hold values from -0.1875 to 0.1875
- value_heads: bfloat16 [1024, 32], P('seq'), may hold values from -0.375 to 0.375
- value_dims: bfloat16 [1024, 128], P('seq'), may hold values from -0.1875 to 0.1875
- out_proj: bfloat16 [1024, 1024], P('seq'), may hold values from -1.5 to 1.5
- ffn_gain: bfloat16 [1024], P('seq'), may hold values from 0.5 to 1.5
- gate_proj: bfloat16 [1024, 2816], P('seq'), may hold values from -0.1875 to 0.1875
- up_proj: bfloat16 [1024, 2816], P('seq'), may hold values from -0.1875 to 0.1875
- down_proj: bfloat16 [2816, 1024], P('seq'), may hold values from -0.109375 to 0.109375
Outputs:
- output: bfloat16 [8, 2048, 1024], P('batch', 'seq')
- input_grad: float32 [8, 2048, 1024], P('batch', 'seq')
- attn_gain_grad: float32 [1024], P('seq')
- query_heads_grad: float32 [1024, 96], P('seq')
- query_dims_grad: float32 [1024, 384], P('seq')
- key_heads_grad: float32 [1024, 32], P('seq')
- key_dims_grad: float32 [1024, 128], P('seq')
- value_heads_grad: float32 [1024, 32], P('seq')
- value_dims_grad: float32 [1024, 128], P('seq')
- out_proj_grad: float32 [1024, 1024], P('seq')
- ffn_gain_grad: float32 [1024], P('seq')
- gate_proj_grad: float32 [1024, 2816], P('seq')
- up_proj_grad: float32 [1024, 2816], P('seq')
- down_proj_grad: float32 [2816, 1024], P('seq')
Inputs may be any that keep to these rules, and one draw needn't show every extreme that they name: `lengths`: in each aligned block of 2 rows (the rows of one index of batch) at least one row has length 2048. `span_order`: the two entries of each row add up to 15 and the first is the smaller; every span number appears once.
All inputs are finite; a program needn't handle non-finite values.
Results may differ from a plain program's by a relative error of at most 0.017.
The roundings to bfloat16 on the way count: a program that leaves them out, or rounds other values in their place, can miss the bound.
Values may be sent and summed in bfloat16 or wider, within the bound.
A program may use at most 320 MiB of HBM per device.

v0:
```python
import math

import jax
import jax.numpy as jnp
from jax import lax
from jax.sharding import PartitionSpec as P

HEADS = 16
HDIM = 64
QRANK = 6
KVRANK = 2


EPSILON = 1e-06
NEG_LARGE = -1e30
HIGH = lax.Precision.HIGHEST


def rms_forward(values, gain):
    scale = lax.rsqrt(jnp.mean(values * values, -1, keepdims=True) + EPSILON)
    unit = values * scale
    return (unit * gain, unit, scale)


def rms_backward(grad_out, unit, scale, gain):
    scaled = grad_out * gain
    grad_in = scale * (scaled - unit * jnp.mean(scaled * unit, -1, keepdims=True))
    return (grad_in, jnp.sum(grad_out * unit, 0))


def rotation(positions):
    half = HDIM // 2
    index = jnp.arange(half).astype(jnp.float32)
    inverse = jnp.exp(index * (-math.log(10000.0) / half))
    angles = positions.astype(jnp.float32)[:, None] * inverse[None, :]
    return (jnp.cos(angles), jnp.sin(angles))


def rotate(vectors, cosine, sine, direction):
    half = HDIM // 2
    first = vectors[..., :half]
    second = vectors[..., half:]
    cos_b = cosine[:, None, :]
    sin_b = direction * sine[:, None, :]
    return jnp.concatenate([first * cos_b - second * sin_b, second * cos_b + first * sin_b], -1)


def outer_sum(left, right):
    return lax.dot_general(
        left, right, (((0,), (0,)), ((), ())), preferred_element_type=jnp.float32
    )


def back_product(grad, weight):
    return lax.dot_general(
        grad, weight, (((1,), (1,)), ((), ())), preferred_element_type=jnp.float32
    )


def forward_dot(left, right):
    return jnp.dot(left, right, preferred_element_type=jnp.float32)


def expand_factors(head_part, dims_part):
    head_full = head_part.reshape(head_part.shape[0], KVRANK, HEADS).astype(jnp.float32)
    dims_full = dims_part.reshape(dims_part.shape[0], KVRANK, HDIM).astype(jnp.float32)
    joined = jnp.einsum("krh,krd->khd", head_full, dims_full, precision=HIGH) / KVRANK
    return (joined.astype(jnp.bfloat16), head_full, dims_full)


def per_device(
    tokens,
    cotangent,
    lengths,
    span_order,
    attn_gain,
    query_heads,
    query_dims,
    key_heads,
    key_dims,
    value_heads,
    value_dims,
    out_proj,
    ffn_gain,
    gate_proj,
    up_proj,
    down_proj,
):
    gathered = (
        lax.all_gather(attn_gain, "seq", axis=0, tiled=True),
        lax.all_gather(query_heads, "seq", axis=0, tiled=True),
        lax.all_gather(query_dims, "seq", axis=0, tiled=True),
        lax.all_gather(key_heads, "seq", axis=0, tiled=True),
        lax.all_gather(key_dims, "seq", axis=0, tiled=True),
        lax.all_gather(value_heads, "seq", axis=0, tiled=True),
        lax.all_gather(value_dims, "seq", axis=0, tiled=True),
        lax.all_gather(out_proj, "seq", axis=0, tiled=True),
        lax.all_gather(ffn_gain, "seq", axis=0, tiled=True),
        lax.all_gather(gate_proj, "seq", axis=0, tiled=True),
        lax.all_gather(up_proj, "seq", axis=0, tiled=True),
        lax.all_gather(down_proj, "seq", axis=0, tiled=True),
    )
    (
        gain_one,
        w_qhead,
        w_qdims,
        w_khead,
        w_kdims,
        w_vhead,
        w_vdims,
        w_output,
        gain_two,
        w_gate,
        w_up,
        w_down,
    ) = gathered
    gain_one = gain_one.astype(jnp.float32)
    gain_two = gain_two.astype(jnp.float32)
    row_count, local_slots, width = tokens.shape
    span = local_slots // 2
    tok_count = row_count * local_slots
    offsets = jnp.arange(span, dtype=jnp.int32)
    own_spans = lax.dynamic_slice_in_dim(span_order, lax.axis_index("seq"), 1, 0)[0]
    local_pos = (own_spans[:, None] * span + offsets[None, :]).reshape(-1)
    key_pos = (span_order.reshape(-1)[:, None] * span + offsets[None, :]).reshape(-1)
    token_pos = jnp.tile(local_pos, row_count)
    cosine, sine = rotation(token_pos)
    flat = tokens.reshape(tok_count, width).astype(jnp.float32)
    normed_full, unit_one, scale_one = rms_forward(flat, gain_one)
    normed = normed_full.astype(jnp.bfloat16)
    q_head_part = forward_dot(normed, w_qhead).reshape(tok_count, QRANK, HEADS)
    q_rotated = rotate(
        forward_dot(normed, w_qdims).reshape(tok_count, QRANK, HDIM), cosine, sine, 1.0
    )
    queries = (jnp.einsum("trh,trd->thd", q_head_part, q_rotated, precision=HIGH) / QRANK).astype(
        jnp.bfloat16
    )
    khead_low = forward_dot(normed, w_khead).astype(jnp.bfloat16)
    kdims_low = rotate(
        forward_dot(normed, w_kdims).reshape(tok_count, KVRANK, HDIM), cosine, sine, 1.0
    ).astype(jnp.bfloat16)
    vhead_low = forward_dot(normed, w_vhead).astype(jnp.bfloat16)
    vdims_low = forward_dot(normed, w_vdims).astype(jnp.bfloat16)
    factor_set = (
        lax.all_gather(khead_low.reshape(row_count, local_slots, -1), "seq", axis=1, tiled=True),
        lax.all_gather(kdims_low.reshape(row_count, local_slots, -1), "seq", axis=1, tiled=True),
        lax.all_gather(vhead_low.reshape(row_count, local_slots, -1), "seq", axis=1, tiled=True),
        lax.all_gather(vdims_low.reshape(row_count, local_slots, -1), "seq", axis=1, tiled=True),
    )
    row_queries = queries.reshape(row_count, local_slots, HEADS, HDIM)

    def row_scores(query_rows, factors, length):
        khead_row, kdims_row, vhead_row, vdims_row = factors
        keys, khead_full, kdims_full = expand_factors(khead_row, kdims_row)
        values, vhead_full, vdims_full = expand_factors(vhead_row, vdims_row)
        raw = (
            jnp.einsum("qhd,khd->hqk", query_rows, keys, preferred_element_type=jnp.float32) * 0.125
        )
        valid = (key_pos[None, :] <= local_pos[:, None]) & (key_pos[None, :] < length)
        scores = jnp.where(valid[None], raw, NEG_LARGE)
        return (scores, keys, values, khead_full, kdims_full, vhead_full, vdims_full)

    def attend_row(args):
        query_rows, factors, length = args
        scores, keys, values = row_scores(query_rows, factors, length)[:3]
        peak = jnp.max(scores, -1, keepdims=True)
        log_total = peak + jnp.log(jnp.sum(jnp.exp(scores - peak), -1, keepdims=True))
        probs = jnp.exp(scores - log_total)
        mixed = jnp.einsum(
            "hqk,khd->qhd", probs.astype(jnp.bfloat16), values, preferred_element_type=jnp.float32
        )
        return (mixed.astype(jnp.bfloat16), log_total)

    heads_out, log_totals = lax.map(attend_row, (row_queries, factor_set, lengths))
    heads_flat = heads_out.reshape(tok_count, width)
    resid = flat + forward_dot(heads_flat, w_output)
    normed_two_full, unit_two, scale_two = rms_forward(resid, gain_two)
    normed_two = normed_two_full.astype(jnp.bfloat16)
    gate = forward_dot(normed_two, w_gate)
    up_part = forward_dot(normed_two, w_up)
    sigma = jax.nn.sigmoid(gate)
    hidden = (gate * sigma * up_part).astype(jnp.bfloat16)
    output = (
        (resid + forward_dot(hidden, w_down))
        .astype(jnp.bfloat16)
        .reshape(row_count, local_slots, width)
    )
    regathered = (
        lax.all_gather(attn_gain, "seq", axis=0, tiled=True),
        lax.all_gather(query_heads, "seq", axis=0, tiled=True),
        lax.all_gather(query_dims, "seq", axis=0, tiled=True),
        lax.all_gather(key_heads, "seq", axis=0, tiled=True),
        lax.all_gather(key_dims, "seq", axis=0, tiled=True),
        lax.all_gather(value_heads, "seq", axis=0, tiled=True),
        lax.all_gather(value_dims, "seq", axis=0, tiled=True),
        lax.all_gather(out_proj, "seq", axis=0, tiled=True),
        lax.all_gather(ffn_gain, "seq", axis=0, tiled=True),
        lax.all_gather(gate_proj, "seq", axis=0, tiled=True),
        lax.all_gather(up_proj, "seq", axis=0, tiled=True),
        lax.all_gather(down_proj, "seq", axis=0, tiled=True),
    )
    w_qhead, w_qdims, w_khead, w_kdims, w_vhead, w_vdims, w_output = regathered[1:8]
    w_gate, w_up, w_down = regathered[9:12]
    grad_out = cotangent.reshape(tok_count, width)
    down_grad = outer_sum(hidden, grad_out)
    d_hidden = back_product(grad_out, w_down)
    d_gate = (d_hidden * up_part * sigma * (1.0 + gate * (1.0 - sigma))).astype(jnp.bfloat16)
    d_up = (d_hidden * gate * sigma).astype(jnp.bfloat16)
    gate_grad = outer_sum(normed_two, d_gate)
    up_grad = outer_sum(normed_two, d_up)
    d_normed_two = back_product(d_gate, w_gate) + back_product(d_up, w_up)
    d_mid, gain_two_grad = rms_backward(d_normed_two, unit_two, scale_two, gain_two)
    d_resid = grad_out.astype(jnp.float32) + d_mid
    d_attn = d_resid.astype(jnp.bfloat16)
    output_grad = outer_sum(heads_flat, d_attn)
    d_heads = (
        back_product(d_attn, w_output)
        .astype(jnp.bfloat16)
        .reshape(row_count, local_slots, HEADS, HDIM)
    )

    def attend_back(args):
        query_rows, factors, length, log_total, head_grads = args
        scores, keys, values, khead_full, kdims_full, vhead_full, vdims_full = row_scores(
            query_rows, factors, length
        )
        probs = jnp.exp(scores - log_total)
        probs_low = probs.astype(jnp.bfloat16)
        d_probs = jnp.einsum("qhd,khd->hqk", head_grads, values, preferred_element_type=jnp.float32)
        spread = jnp.sum(probs * d_probs, -1, keepdims=True)
        d_scores = (probs * (d_probs - spread)).astype(jnp.bfloat16)
        d_queries = (
            jnp.einsum("hqk,khd->qhd", d_scores, keys, preferred_element_type=jnp.float32) * 0.125
        )
        d_keys = (
            jnp.einsum("hqk,qhd->khd", d_scores, query_rows, preferred_element_type=jnp.float32)
            * 0.125
        )
        d_values = jnp.einsum(
            "hqk,qhd->khd", probs_low, head_grads, preferred_element_type=jnp.float32
        )
        dk_head = jnp.einsum("khd,krd->krh", d_keys, kdims_full, precision=HIGH) / KVRANK
        dk_dims = jnp.einsum("khd,krh->krd", d_keys, khead_full, precision=HIGH) / KVRANK
        dv_head = jnp.einsum("khd,krd->krh", d_values, vdims_full, precision=HIGH) / KVRANK
        dv_dims = jnp.einsum("khd,krh->krd", d_values, vhead_full, precision=HIGH) / KVRANK
        slots = dk_head.shape[0]
        return (
            d_queries,
            dk_head.reshape(slots, -1),
            dk_dims.reshape(slots, -1),
            dv_head.reshape(slots, -1),
            dv_dims.reshape(slots, -1),
        )

    d_queries, dk_head_all, dk_dims_all, dv_head_all, dv_dims_all = lax.map(
        attend_back, (row_queries, factor_set, lengths, log_totals, d_heads)
    )
    dk_head_own, dk_dims_own, dv_head_own, dv_dims_own = (
        lax.psum_scatter(dk_head_all, "seq", scatter_dimension=1, tiled=True),
        lax.psum_scatter(dk_dims_all, "seq", scatter_dimension=1, tiled=True),
        lax.psum_scatter(dv_head_all, "seq", scatter_dimension=1, tiled=True),
        lax.psum_scatter(dv_dims_all, "seq", scatter_dimension=1, tiled=True),
    )
    d_queries = d_queries.reshape(tok_count, HEADS, HDIM)
    dq_head = (
        (jnp.einsum("thd,trd->trh", d_queries, q_rotated, precision=HIGH) / QRANK)
        .astype(jnp.bfloat16)
        .reshape(tok_count, -1)
    )
    dq_rotated = jnp.einsum("thd,trh->trd", d_queries, q_head_part, precision=HIGH) / QRANK
    dq_dims = rotate(dq_rotated, cosine, sine, -1.0).astype(jnp.bfloat16).reshape(tok_count, -1)
    dk_head_low = dk_head_own.reshape(tok_count, -1).astype(jnp.bfloat16)
    dk_dims_low = (
        rotate(dk_dims_own.reshape(tok_count, KVRANK, HDIM), cosine, sine, -1.0)
        .astype(jnp.bfloat16)
        .reshape(tok_count, -1)
    )
    dv_head_low = dv_head_own.reshape(tok_count, -1).astype(jnp.bfloat16)
    dv_dims_low = dv_dims_own.reshape(tok_count, -1).astype(jnp.bfloat16)
    factor_pairs = (
        (dq_head, w_qhead),
        (dq_dims, w_qdims),
        (dk_head_low, w_khead),
        (dk_dims_low, w_kdims),
        (dv_head_low, w_vhead),
        (dv_dims_low, w_vdims),
    )
    factor_grads = [outer_sum(normed, grad_part) for grad_part, weight in factor_pairs]
    d_normed = back_product(dq_head, w_qhead)
    for grad_part, weight in factor_pairs[1:]:
        d_normed = d_normed + back_product(grad_part, weight)
    d_first, gain_one_grad = rms_backward(d_normed, unit_one, scale_one, gain_one)
    input_grad = (d_resid + d_first).reshape(row_count, local_slots, width)
    summed = (
        lax.psum_scatter(gain_one_grad, "seq", scatter_dimension=0, tiled=True),
        lax.psum_scatter(factor_grads[0], "seq", scatter_dimension=0, tiled=True),
        lax.psum_scatter(factor_grads[1], "seq", scatter_dimension=0, tiled=True),
        lax.psum_scatter(factor_grads[2], "seq", scatter_dimension=0, tiled=True),
        lax.psum_scatter(factor_grads[3], "seq", scatter_dimension=0, tiled=True),
        lax.psum_scatter(factor_grads[4], "seq", scatter_dimension=0, tiled=True),
        lax.psum_scatter(factor_grads[5], "seq", scatter_dimension=0, tiled=True),
        lax.psum_scatter(output_grad, "seq", scatter_dimension=0, tiled=True),
        lax.psum_scatter(gain_two_grad, "seq", scatter_dimension=0, tiled=True),
        lax.psum_scatter(gate_grad, "seq", scatter_dimension=0, tiled=True),
        lax.psum_scatter(up_grad, "seq", scatter_dimension=0, tiled=True),
        lax.psum_scatter(down_grad, "seq", scatter_dimension=0, tiled=True),
    )
    totals = (
        lax.psum(summed[0].astype(jnp.bfloat16), "batch").astype(jnp.float32),
        lax.psum(summed[1].astype(jnp.bfloat16), "batch").astype(jnp.float32),
        lax.psum(summed[2].astype(jnp.bfloat16), "batch").astype(jnp.float32),
        lax.psum(summed[3].astype(jnp.bfloat16), "batch").astype(jnp.float32),
        lax.psum(summed[4].astype(jnp.bfloat16), "batch").astype(jnp.float32),
        lax.psum(summed[5].astype(jnp.bfloat16), "batch").astype(jnp.float32),
        lax.psum(summed[6].astype(jnp.bfloat16), "batch").astype(jnp.float32),
        lax.psum(summed[7].astype(jnp.bfloat16), "batch").astype(jnp.float32),
        lax.psum(summed[8].astype(jnp.bfloat16), "batch").astype(jnp.float32),
        lax.psum(summed[9].astype(jnp.bfloat16), "batch").astype(jnp.float32),
        lax.psum(summed[10].astype(jnp.bfloat16), "batch").astype(jnp.float32),
        lax.psum(summed[11].astype(jnp.bfloat16), "batch").astype(jnp.float32),
    )
    return (
        output,
        input_grad,
        totals[0],
        totals[1],
        totals[2],
        totals[3],
        totals[4],
        totals[5],
        totals[6],
        totals[7],
        totals[8],
        totals[9],
        totals[10],
        totals[11],
    )


def solution(mesh):
    return jax.shard_map(
        per_device,
        mesh=mesh,
        in_specs=(
            P("batch", "seq", None),
            P("batch", "seq", None),
            P("batch"),
            P(),
            P("seq"),
            P("seq", None),
            P("seq", None),
            P("seq", None),
            P("seq", None),
            P("seq", None),
            P("seq", None),
            P("seq", None),
            P("seq"),
            P("seq", None),
            P("seq", None),
            P("seq", None),
        ),
        out_specs=(
            P("batch", "seq", None),
            P("batch", "seq", None),
            P("seq"),
            P("seq", None),
            P("seq", None),
            P("seq", None),
            P("seq", None),
            P("seq", None),
            P("seq", None),
            P("seq", None),
            P("seq"),
            P("seq", None),
            P("seq", None),
            P("seq", None),
        ),
        check_vma=False,
    )
```

profile of v0, /device:TPU:0, one launch (start us, length us, event | category | flops | bytes accessed | tf_op | source)
XLA Modules:
  0.0 2521.6 jit_solution(16951029878545555751)
XLA Ops:
  7.2 22.3 all-gather
  31.1 31.1 %all_gather.61 = bf16[1024,128]{1,0:T(8,128)(2,1)S(1)} all-gather(bf16[128,128]{1,0:T(8,128)(2,1)} %param.30), channel_id=1, replica_groups=mesh['seq'=8,'batch'=4] {'seq'}, dimensions={0}, use_global_device_ids=true | all-gather | bytes 294912 | tf_op jit(solution)/shard_map/all_gather | solution.py:96
  65.5 31.0 %all_gather.67 = bf16[1024,128]{1,0:T(8,128)(2,1)S(1)} all-gather(bf16[128,128]{1,0:T(8,128)(2,1)S(1)} %copy-done.60), channel_id=1, replica_groups=mesh['seq'=8,'batch'=4] {'seq'}, dimensions={0}, use_global_device_ids=true | all-gather | bytes 294912 | tf_op jit(solution)/shard_map/all_gather | solution.py:94
  101.9 26.0 %all_gather.59 = bf16[1024,32]{0,1:T(8,128)(2,1)S(1)} all-gather(bf16[128,32]{0,1:T(8,128)(2,1)S(1)} %copy-done.64), channel_id=1, replica_groups=mesh['seq'=8,'batch'=4] {'seq'}, dimensions={0}, use_global_device_ids=true | all-gather | bytes 73728 | tf_op jit(solution)/shard_map/all_gather | solution.py:95
  128.5 31.3 %all_gather.60 = bf16[2,2048,32]{1,2,0:T(8,128)(2,1)S(1)} all-gather(bf16[2,256,32]{1,2,0:T(8,128)(2,1)S(1)} %bitcast.369), channel_id=1, replica_groups=mesh['seq'=8,'batch'=4] {'seq'}, dimensions={1}, use_global_device_ids=true | all-gather | bytes 294912 | tf_op jit(solution)/shard_map/all_gather | solution.py:147
  159.9 27.6 %all_gather.63 = bf16[1024,96]{0,1:T(8,128)(2,1)S(1)} all-gather(bf16[128,96]{0,1:T(8,128)(2,1)S(1)} %copy-done.63), channel_id=1, replica_groups=mesh['seq'=8,'batch'=4] {'seq'}, dimensions={0}, use_global_device_ids=true | all-gather | bytes 221184 | tf_op jit(solution)/shard_map/all_gather | solution.py:91
  191.0 35.7 %all_gather.64 = bf16[1024,384]{1,0:T(8,128)(2,1)} all-gather(bf16[128,384]{1,0:T(8,128)(2,1)} %param.26), channel_id=1, replica_groups=mesh['seq'=8,'batch'=4] {'seq'}, dimensions={0}, use_global_device_ids=true | all-gather | bytes 884736 | tf_op jit(solution)/shard_map/all_gather | solution.py:92
  245.6 27.1 %all_gather.65 = bf16[1024,32]{0,1:T(8,128)(2,1)S(1)} all-gather(bf16[128,32]{0,1:T(8,128)(2,1)S(1)} %copy-done.65), channel_id=1, replica_groups=mesh['seq'=8,'batch'=4] {'seq'}, dimensions={0}, use_global_device_ids=true | all-gather | bytes 73728 | tf_op jit(solution)/shard_map/all_gather | solution.py:93
  273.1 31.6 %all_gather.66 = bf16[2,2048,32]{1,2,0:T(8,128)(2,1)S(1)} all-gather(bf16[2,256,32]{1,2,0:T(8,128)(2,1)S(1)} %bitcast.371), channel_id=1, replica_groups=mesh['seq'=8,'batch'=4] {'seq'}, dimensions={1}, use_global_device_ids=true | all-gather | bytes 294912 | tf_op jit(solution)/shard_map/all_gather | solution.py:145
  321.9 144.9 %while.32 = (s32[]{:T(128)}, bf16[2,256,16,64]{1,3,2,0:T(8,128)(2,1)}, f32[2,16,256,1]{2,1,3,0:T(8,128)S(1)}, bf16[2,2048,32]{1,2,0:T(8,128)(2,1)S(1)}, bf16[2,2...) while((s32[]{:T(128)}, ...), condition=%wide.region_4.5_spmd.clone, body=%wide.region_1.4_spmd.clone.sunk | while | flops 2266237184 | bytes 141973904 | solution.py:174
  334.7 18.2 fusion.209
  520.1 553.9 %while.33 = (s32[]{:T(128)}, f32[2,256,16,64]{1,3,2,0:T(8,128)}, f32[2,2048,32]{1,2,0:T(8,128)}, f32[2,2048,128]{1,2,0:T(8,128)}, f32[2,2048,32]{1,2,0:T(8,128)}...) while((s32[]{:T(128)}, f32[2,256,16,64]{1,3,2,0:T(8,128)}, ...), condition=%wide.region_9.10_spmd.clone, body=%wide.region_7.9_spmd.clone.sunk | while | flops 5678958592 | bytes 450992704 | solution.py:255
  608.4 28.6 %multiply_reduce_fusion.6 = (f32[16,256]{1,0:T(8,128)S(1)}, f32[16,256,2048]{2,1,0:T(8,128)}) fusion(f32[16,256,2048]{2,1,0:T(8,128)} %fusion.230, f32[16,256]{1,0:T(8,128)S(1)} %dynamic-slice_bitcast_fusion.2, f32[2048,16,64]{0,2,1:T(8,128)} %copy.314, bf16[2,256,16,64]{1,3,2,0:T(8,128)(2,1)} %get-tuple-element.735, s32[]{:T(128)S(6)} %copy.344, ...), kind=kOutput, calls=%fused_computation.34.clone.1 | convolution fusion | flops 1119875072 | bytes 76578816 | tf_op jit(solution)/shard_map/while/body/eval_jaxpr/qhd,khd->hqk/dot_general | solution.py:157
  636.9 27.4 %multiply_convert_fusion.29 = bf16[16,256,2048]{2,1,0:T(8,128)(2,1)} fusion(f32[16,256,2048]{2,1,0:T(8,128)} %get-tuple-element.652, f32[16,256,2048]{2,1,0:T(8,128)} %fusion.230, f32[16,256]{1,0:T(8,128)S(1)} %get-tuple-element.653), kind=kLoop, calls=%fused_computation.33.clone.1 | loop fusion | flops 25165824 | bytes 83902464 | tf_op jit(solution)/shard_map/while/body/eval_jaxpr/convert_element_type | solution.py:231
  870.4 28.6 %multiply_reduce_fusion.6 = (f32[16,256]{1,0:T(8,128)S(1)}, f32[16,256,2048]{2,1,0:T(8,128)}) fusion(f32[16,256,2048]{2,1,0:T(8,128)} %fusion.230, f32[16,256]{1,0:T(8,128)S(1)} %dynamic-slice_bitcast_fusion.2, f32[2048,16,64]{0,2,1:T(8,128)} %copy.314, bf16[2,256,16,64]{1,3,2,0:T(8,128)(2,1)} %get-tuple-element.735, s32[]{:T(128)S(6)} %copy.344, ...), kind=kOutput, calls=%fused_computation.34.clone.1 | convolution fusion | flops 1119875072 | bytes 76578816 | tf_op jit(solution)/shard_map/while/body/eval_jaxpr/qhd,khd->hqk/dot_general | solution.py:157
  899.0 27.4 %multiply_convert_fusion.29 = bf16[16,256,2048]{2,1,0:T(8,128)(2,1)} fusion(f32[16,256,2048]{2,1,0:T(8,128)} %get-tuple-element.652, f32[16,256,2048]{2,1,0:T(8,128)} %fusion.230, f32[16,256]{1,0:T(8,128)S(1)} %get-tuple-element.653), kind=kLoop, calls=%fused_computation.33.clone.1 | loop fusion | flops 25165824 | bytes 83902464 | tf_op jit(solution)/shard_map/while/body/eval_jaxpr/convert_element_type | solution.py:231
  1093.9 41.5 %reduce-scatter.15.cloned.1.call-done = f32[2,256,32]{1,2,0:T(8,128)} async-done(((f32[2,2048,32]{1,2,0:T(8,128)}), f32[2,256,32]{1,2,0:T(8,128)}) %reduce-scatter.15.cloned.1.call-update) | async-done | bytes 65552 | tf_op jit(solution)/shard_map/reduce_scatter | solution.py:259
  1137.2 63.2 %reduce-scatter.19.cloned.1.call-done = f32[2,256,32]{1,2,0:T(8,128)} async-done(((f32[2,2048,32]{1,2,0:T(8,128)}), f32[2,256,32]{1,2,0:T(8,128)}) %reduce-scatter.19.cloned.1.call-update) | async-done | bytes 65552 | tf_op jit(solution)/shard_map/reduce_scatter | solution.py:261
  1202.3 69.0 %reduce-scatter.17.cloned.1.call-done = f32[2,256,128]{1,2,0:T(8,128)} async-done(((f32[2,2048,128]{1,2,0:T(8,128)}), f32[2,256,128]{1,2,0:T(8,128)}) %reduce-scatter.17.cloned.1.call-update) | async-done | bytes 262160 | tf_op jit(solution)/shard_map/reduce_scatter | solution.py:260
  1274.8 66.7 %reduce-scatter.21.cloned.1.call-done = f32[2,256,128]{2,1,0:T(8,128)} async-done(((f32[2,2048,128]{2,1,0:T(8,128)}), f32[2,256,128]{2,1,0:T(8,128)}) %reduce-scatter.21.cloned.1.call-update) | async-done | bytes 262160 | tf_op jit(solution)/shard_map/reduce_scatter | solution.py:262
  1411.2 58.8 %reduce-scatter.27.cloned.1.call-done = f32[128,32]{0,1:T(8,128)} async-done(((f32[1024,32]{0,1:T(8,128)}), f32[128,32]{0,1:T(8,128)}) %reduce-scatter.27.cloned.1.call-update) | async-done | bytes 16400 | tf_op jit(solution)/shard_map/reduce_scatter | solution.py:298
  1471.3 62.3 %reduce-scatter.31.cloned.1.call-done = f32[128,32]{0,1:T(8,128)} async-done(((f32[1024,32]{0,1:T(8,128)}), f32[128,32]{0,1:T(8,128)}) %reduce-scatter.31.cloned.1.call-update) | async-done | bytes 16400 | tf_op jit(solution)/shard_map/reduce_scatter | solution.py:300
  1541.3 19.8 all-reduce.2
  1562.3 36.1 %reduce-scatter.29.cloned.1.call-done = f32[128,128]{1,0:T(8,128)} async-done(((f32[1024,128]{1,0:T(8,128)}), f32[128,128]{1,0:T(8,128)}) %reduce-scatter.29.cloned.1.call-update) | async-done | bytes 65552 | tf_op jit(solution)/shard_map/reduce_scatter | solution.py:299
  1599.9 63.7 %reduce-scatter.33.cloned.1.call-done = f32[128,128]{1,0:T(8,128)} async-done(((f32[1024,128]{1,0:T(8,128)}), f32[128,128]{1,0:T(8,128)}) %reduce-scatter.33.cloned.1.call-update) | async-done | bytes 65552 | tf_op jit(solution)/shard_map/reduce_scatter | solution.py:301
  1665.1 65.6 %reduce-scatter.25.cloned.1.call-done = f32[128,384]{1,0:T(8,128)} async-done(((f32[1024,384]{1,0:T(8,128)}), f32[128,384]{1,0:T(8,128)}) %reduce-scatter.25.cloned.1.call-update) | async-done | bytes 196624 | tf_op jit(solution)/shard_map/reduce_scatter | solution.py:297
  1732.3 89.2 %reduce-scatter.35.cloned.1.call-done = f32[128,1024]{1,0:T(8,128)} async-done(((f32[1024,1024]{1,0:T(8,128)}), f32[128,1024]{1,0:T(8,128)}) %reduce-scatter.35.cloned.1.call-update) | async-done | bytes 524304 | tf_op jit(solution)/shard_map/reduce_scatter | solution.py:302
  1823.3 194.0 %reduce-scatter.37.cloned.1.call-done = f32[128,2816]{1,0:T(8,128)} async-done(((f32[1024,2816]{1,0:T(8,128)}), f32[128,2816]{1,0:T(8,128)}) %reduce-scatter.37.cloned.1.call-update) | async-done | bytes 1441808 | tf_op jit(solution)/shard_map/reduce_scatter | solution.py:304
  2019.5 193.1 %reduce-scatter.39.cloned.1.call-done = f32[128,2816]{1,0:T(8,128)} async-done(((f32[1024,2816]{1,0:T(8,128)}), f32[128,2816]{1,0:T(8,128)}) %reduce-scatter.39.cloned.1.call-update) | async-done | bytes 1441808 | tf_op jit(solution)/shard_map/reduce_scatter | solution.py:305
  2215.0 193.0 %reduce-scatter.41.cloned.1.call-done = f32[352,1024]{1,0:T(8,128)} async-done(((f32[2816,1024]{1,0:T(8,128)}), f32[352,1024]{1,0:T(8,128)}) %reduce-scatter.41.cloned.1.call-update) | async-done | bytes 1441808 | tf_op jit(solution)/shard_map/reduce_scatter | solution.py:306
  2419.9 21.4 all-reduce.8.cloned.1.call-done
  2450.5 55.8 %all-reduce.10.cloned.1.call-done = (bf16[128,384]{1,0:T(8,128)(2,1)}, bf16[128,1024]{1,0:T(8,128)(2,1)}, bf16[128,2816]{1,0:T(8,128)(2,1)}, bf16[128,2816]{1,0:T(8,128)(2,1)}, bf16[352,1024]{1,0:T(8,128)(2,1)}) async-done(((bf16[128,384]{1,0:T(8,128)(2,1)}, bf16[128,1024]{1,0:T(8,128)(2,1)}, bf16[128,2816]{1,0:T(8,128)(2,1)}, bf16[128,2816]{1,0:T(8,128)(2,1)}, bf16[352,1024]{1,0:T(8,128)(2,1)}), ...) | async-done | bytes 2523152 | tf_op jit(solution)/shard_map/psum | solution.py:311
  (450 shorter events, 787.8 us)
Async XLA Ops:
  7.2 314.7 %all-gather.9.cloned.1.call-start = ((), (), s32[]{:S(2)}) async-start(), calls=%async_computation.14 | async-start | bytes 1179648 | tf_op jit(solution)/shard_map/all_gather | solution.py:148
  65.1 256.8 %all-gather.11.cloned.1.call-start = ((), (), s32[]{:S(2)}) async-start(), calls=%async_computation.15 | async-start | bytes 1179648 | tf_op jit(solution)/shard_map/all_gather | solution.py:146
  97.6 133.0 %copy-start.33 = (f32[512,32]{0,1:T(8,128)}, f32[512,32]{0,1:T(8,128)S(1)}, u32[]{:S(2)}) copy-start(f32[512,32]{0,1:T(8,128)S(1)} %get-tuple-element.461) | copy-start | bytes 196612
  98.0 130.9 %copy-start.2 = (bf16[2,256,1024]{2,1,0:T(8,128)(2,1)}, bf16[2,256,1024]{2,1,0:T(8,128)(2,1)S(1)}, u32[]{:S(2)}) copy-start(bf16[2,256,1024]{2,1,0:T(8,128)(2,1)S(1)} %fusion.66) | copy-start | bytes 3145732
  99.3 371.2 %all-gather.13.cloned.1.call-start = ((), (), s32[]{:S(2)}) async-start(), calls=%async_computation.16 | async-start | bytes 2359296 | tf_op jit(solution)/shard_map/all_gather | solution.py:97
  100.0 374.1 %all-gather.15.cloned.1.call-start = ((), (), s32[]{:S(2)}) async-start(), calls=%async_computation.17 | async-start | bytes 6488064 | tf_op jit(solution)/shard_map/all_gather | solution.py:99
  100.6 381.9 %all-gather.17.cloned.1.call-start = ((), (), s32[]{:S(2)}) async-start(), calls=%async_computation.18 | async-start | bytes 6488064 | tf_op jit(solution)/shard_map/all_gather | solution.py:100
  101.2 388.8 %all-gather.19.cloned.1.call-start = ((), (), s32[]{:S(2)}) async-start(), calls=%async_computation.19 | async-start | bytes 6488064 | tf_op jit(solution)/shard_map/all_gather | solution.py:101
  101.8 1033.6 %reduce-scatter.15.cloned.1.call-start = ((), (), s32[]{:S(2)}) async-start(), calls=%async_computation.20 | async-start | bytes 589824 | tf_op jit(solution)/shard_map/reduce_scatter | solution.py:259
  1074.0 126.4 %reduce-scatter.19.cloned.1.call-start = ((), (), s32[]{:S(2)}) async-start(), calls=%async_computation.22 | async-start | bytes 589824 | tf_op jit(solution)/shard_map/reduce_scatter | solution.py:261
  1074.8 196.6 %reduce-scatter.17.cloned.1.call-start = ((), (), s32[]{:S(2)}) async-start(), calls=%async_computation.21 | async-start | bytes 2359296 | tf_op jit(solution)/shard_map/reduce_scatter | solution.py:260
  1075.5 266.0 %reduce-scatter.21.cloned.1.call-start = ((), (), s32[]{:S(2)}) async-start(), calls=%async_computation.23 | async-start | bytes 2359296 | tf_op jit(solution)/shard_map/reduce_scatter | solution.py:262
  1076.1 330.4 %reduce-scatter.23.cloned.1.call-start = ((), (), s32[]{:S(2)}) async-start(), calls=%async_computation.24 | async-start | bytes 442368 | tf_op jit(solution)/shard_map/reduce_scatter | solution.py:296
  1092.7 180.0 %copy-start.34 = (f32[512,32]{0,1:T(8,128)S(1)}, f32[512,32]{0,1:T(8,128)}, u32[]{:S(2)}) copy-start(f32[512,32]{0,1:T(8,128)} %copy-done.33) | copy-start | bytes 196612
  1092.7 180.0 %copy-start.51 = (f32[512,32]{0,1:T(8,128)S(1)}, f32[512,32]{0,1:T(8,128)}, u32[]{:S(2)}) copy-start(f32[512,32]{0,1:T(8,128)} %get-tuple-element.459) | copy-start | bytes 196612
  1093.8 376.2 %reduce-scatter.27.cloned.1.call-start = ((), (), s32[]{:S(2)}) async-start(), calls=%async_computation.26 | async-start | bytes 147456 | tf_op jit(solution)/shard_map/reduce_scatter | solution.py:298
  1137.2 396.5 %reduce-scatter.31.cloned.1.call-start = ((), (), s32[]{:S(2)}) async-start(), calls=%async_computation.28 | async-start | bytes 147456 | tf_op jit(solution)/shard_map/reduce_scatter | solution.py:300
  1202.3 396.2 %reduce-scatter.29.cloned.1.call-start = ((), (), s32[]{:S(2)}) async-start(), calls=%async_computation.27 | async-start | bytes 589824 | tf_op jit(solution)/shard_map/reduce_scatter | solution.py:299
  1274.8 388.8 %reduce-scatter.33.cloned.1.call-start = ((), (), s32[]{:S(2)}) async-start(), calls=%async_computation.29 | async-start | bytes 589824 | tf_op jit(solution)/shard_map/reduce_scatter | solution.py:301
  1344.4 386.3 %reduce-scatter.25.cloned.1.call-start = ((), (), s32[]{:S(2)}) async-start(), calls=%async_computation.25 | async-start | bytes 1769472 | tf_op jit(solution)/shard_map/reduce_scatter | solution.py:297
  1355.1 466.4 %reduce-scatter.35.cloned.1.call-start = ((), (), s32[]{:S(2)}) async-start(), calls=%async_computation.30 | async-start | bytes 4718592 | tf_op jit(solution)/shard_map/reduce_scatter | solution.py:302
  1359.6 657.6 %reduce-scatter.37.cloned.1.call-start = ((), (), s32[]{:S(2)}) async-start(), calls=%async_computation.31 | async-start | bytes 12976128 | tf_op jit(solution)/shard_map/reduce_scatter | solution.py:304
  1368.8 843.9 %reduce-scatter.39.cloned.1.call-start = ((), (), s32[]{:S(2)}) async-start(), calls=%async_computation.32 | async-start | bytes 12976128 | tf_op jit(solution)/shard_map/reduce_scatter | solution.py:305
  1376.6 1031.3 %reduce-scatter.41.cloned.1.call-start = ((), (), s32[]{:S(2)}) async-start(), calls=%async_computation.33 | async-start | bytes 12976128 | tf_op jit(solution)/shard_map/reduce_scatter | solution.py:306
  1385.7 1055.7 %all-reduce.8.cloned.1.call-start = ((), (), s32[]{:S(2)}) async-start(), calls=%async_computation.34 | async-start | bytes 215040 | tf_op jit(solution)/shard_map/psum | solution.py:309
  1391.0 145.6 %copy-start.29 = (bf16[1024,128]{1,0:T(8,128)(2,1)S(1)}, bf16[1024,128]{1,0:T(8,128)(2,1)}, u32[]{:S(2)}) copy-start(bf16[1024,128]{1,0:T(8,128)(2,1)} %copy-done.28) | copy-start | bytes 786436
  1391.0 145.6 %copy-start.36 = (bf16[2,256,128]{2,1,0:T(8,128)(2,1)S(1)}, bf16[2,256,128]{2,1,0:T(8,128)(2,1)}, u32[]{:S(2)}) copy-start(bf16[2,256,128]{2,1,0:T(8,128)(2,1)} %copy-done.35) | copy-start | bytes 393220
  1411.2 125.9 %copy-start.7 = (bf16[2,256,1024]{2,1,0:T(8,128)(2,1)S(1)}, bf16[2,256,1024]{2,1,0:T(8,128)(2,1)}, u32[]{:S(2)}) copy-start(bf16[2,256,1024]{2,1,0:T(8,128)(2,1)} %param.20) | copy-start | bytes 3145732
  1411.2 125.9 %copy-start.58 = (f32[8,1,128]{2,1,0:T(1,128)S(1)}, f32[8,1,128]{2,1,0:T(1,128)}, u32[]{:S(2)}) copy-start(f32[8,1,128]{2,1,0:T(1,128)} %copy-done.57) | copy-start | bytes 12292
  1411.2 125.9 %copy-start.62 = (f32[1,2,2,128]{3,1,2,0:T(2,128)S(1)}, f32[1,2,2,128]{3,1,2,0:T(2,128)}, u32[]{:S(2)}) copy-start(f32[1,2,2,128]{3,1,2,0:T(2,128)} %copy-done.61) | copy-start | bytes 6148
  1665.0 841.2 %all-reduce.10.cloned.1.call-start = ((), (), s32[]{:S(2)}) async-start(), calls=%async_computation.35 | async-start | bytes 5046272 | tf_op jit(solution)/shard_map/psum | solution.py:311
  2215.0 195.3 %copy-start.12 = (f32[512,1024]{1,0:T(8,128)S(1)}, f32[512,1024]{1,0:T(8,128)}, u32[]{:S(2)}) copy-start(f32[512,1024]{1,0:T(8,128)} %copy-done.11) | copy-start | bytes 6291460
  (76 other events, 1385.2 us)
Sparse Core Ops, SparseCore 0:
  65.3 38.7 all-gather.8
  106.1 40.2 all-gather.10
  148.5 52.9 all-gather.12
  203.5 96.7 all-gather.14
  302.3 91.2 all-gather.16
  395.6 90.8 all-gather.18
  1074.2 61.1 reduce-scatter.14
  1139.1 61.3 reduce-scatter.18
  1204.0 67.3 reduce-scatter.16
  1274.7 66.7 reduce-scatter.20
  1345.4 61.1 reduce-scatter.22
  1409.7 60.2 reduce-scatter.26
  1473.3 60.2 reduce-scatter.30
  1537.4 60.9 reduce-scatter.28
  1602.6 60.9 reduce-scatter.32
  1666.8 63.8 reduce-scatter.24
  1734.6 86.8 reduce-scatter.34
  1824.9 192.2 reduce-scatter.36
  2020.8 191.8 reduce-scatter.38
  2216.1 191.7 reduce-scatter.40
  2411.9 29.3 all-reduce.7
  2445.5 60.7 all-reduce.9
where the time goes:
time: 2530 us; the launch traced here: 2520 us
  waiting for transfers between devices  1290 us (51%)
  matrix products  539 us (21%)
  blocking collectives  300 us (12%)
  local copies, waits for them, and re-layouts  206 us (8%)
  other arithmetic  135 us (5%)
  loops' own time  30.5 us (1%)
    reduce_scatter x1, waiting for transfers between devices, per_device(): lax.psum_scatter(gate_grad, 'seq', scatter_dimension=0, tiled=True)  194 us
    reduce_scatter x1, waiting for transfers between devices, per_device(): lax.psum_scatter(up_grad, 'seq', scatter_dimension=0, tiled=True)  193 us
    reduce_scatter x1, waiting for transfers between devices, per_device(): lax.psum_scatter(down_grad, 'seq', scatter_dimension=0, tiled=True)  193 us
    dot_general x4, matrix products, row_scores(): jnp.einsum('qhd,khd->hqk', query_rows, keys, preferred_element_type=jnp.f...  93.5 us
    reduce_scatter x1, waiting for transfers between devices, per_device(): lax.psum_scatter(output_grad, 'seq', scatter_dimension=0, tiled=True)  89.2 us
    reduce_scatter x1, waiting for transfers between devices, per_device(): lax.psum_scatter(dk_dims_all, 'seq', scatter_dimension=1, tiled=True)  69 us
    reduce_scatter x1, waiting for transfers between devices, per_device(): lax.psum_scatter(dv_dims_all, 'seq', scatter_dimension=1, tiled=True)  66.7 us
    reduce_scatter x1, waiting for transfers between devices, per_device(): lax.psum_scatter(factor_grads[1], 'seq', scatter_dimension=0, tiled=True)  65.6 us
  transfers between devices with their start and end apart: 22, of which 16 were waited for; matrix products, arithmetic and copies ran while one was open for 12% of the time, Pallas kernels for 0%

commit v1 on v0

v1 whole, which is shorter than its diff:
```python
import functools
import math

import jax
import jax.numpy as jnp
from jax import lax
from jax.experimental import pallas as pl
from jax.experimental.pallas import tpu as pltpu
from jax.sharding import PartitionSpec as P


MESH = pl.DeviceIdType.MESH
NZ, NX = 4, 2

class Place:
    def __init__(self):
        self.seq = lax.axis_index("seq")
        self.batch = lax.axis_index("batch")
        self.z = self.seq // 2
        self.x = lax.rem(self.seq, 2)
        self.y = self.batch // 2
        self.c = lax.rem(self.batch, 2)
        self.up = (jnp.minimum(self.seq + 2, 7), self.batch)
        self.down = (jnp.maximum(self.seq - 2, 0), self.batch)
        self.xp = (self.seq + 1 - 2 * self.x, self.batch)
        self.yp = (self.seq, lax.rem(self.batch + 2, 4))
        self.cp = (self.seq, self.batch + 1 - 2 * self.c)

def greet(me):
    bar = pltpu.get_barrier_semaphore()
    def sig(d):
        pl.semaphore_signal(bar, inc=1, device_id=d, device_id_type=MESH)
    pl.when(me.z < NZ - 1)(lambda: sig(me.up))
    pl.when(me.z > 0)(lambda: sig(me.down))
    sig(me.xp); sig(me.yp); sig(me.cp)
    ends = (me.z == 0) | (me.z == NZ - 1)
    pl.semaphore_wait(bar, jnp.where(ends, 4, 5))

def piece(ref, spec, y, c):
    flow, axis, size = spec
    part = (2 * y + c, size // 4) if flow == "P" else (c, size // 2)
    start = pl.multiple_of(part[0] * part[1], part[1])
    idx = [slice(None)] * 2
    idx[axis] = pl.ds(start, part[1])
    return ref.at[tuple(idx)]

def gather_kernel(specs, order, *refs):
    n = len(specs)
    ins, outs = refs[:n], refs[n:2 * n]
    zs, zr, xs, xr, ys, yr, cs, cr, ls = refs[2 * n:]
    me = Place()
    greet(me)
    sends = []
    def remote(cond, src, dst, ss, rs, dev):
        cp = lambda: pltpu.make_async_remote_copy(src_ref=src, dst_ref=dst, send_sem=ss, recv_sem=rs, device_id=dev, device_id_type=MESH)
        if cond is None:
            cp().start()
        else:
            pl.when(cond)(lambda: cp().start())
        sends.append((cond, cp))
    def recv(src, dst, rs, dev):
        pltpu.make_async_remote_copy(src_ref=dst, dst_ref=dst, send_sem=rs, recv_sem=rs, device_id=dev, device_id_type=MESH).wait_recv()
    def view(a, shard, y, c):
        return piece(outs[a].at[shard], specs[a], y, c)
    own = [piece(ins[a], specs[a], me.y, me.c) for a in range(n)]
    for a in order:
        dst = view(a, me.seq, me.y, me.c)
        remote(me.z < NZ - 1, own[a], dst, zs.at[a, 0, 0], zr.at[a, 0, 0], me.up)
        remote(me.z > 0, own[a], dst, zs.at[a, 1, 0], zr.at[a, 1, 0], me.down)
        remote(None, own[a], dst, xs.at[a, me.z], xr.at[a, me.z], me.xp)
    for a in range(n):
        pltpu.make_async_copy(ins[a], outs[a].at[me.seq], ls.at[a]).start()
    def onward(a, shard, cond, wave):
        v = view(a, shard, me.y, me.c)
        if specs[a][0] == "P":
            remote(cond, v, v, ys.at[a, shard], yr.at[a, shard], me.yp)
        remote(cond, v, v, cs.at[a, 0, shard], cr.at[a, 0, shard], me.cp)
    def zstep(a, k):
        for d, (cond, zz, frm, fwd_ok, to) in enumerate((
            (me.z - k >= 0, me.z - k, me.down, me.z < NZ - 1, me.up),
            (me.z + k < NZ, me.z + k, me.up, me.z > 0, me.down))):
            zz = jnp.clip(zz, 0, NZ - 1)
            shard = 2 * zz + me.x
            v = view(a, shard, me.y, me.c)
            pl.when(cond)(lambda: recv(v, v, zr.at[a, d, k - 1], frm))
            if k < NZ - 1:
                remote(cond & fwd_ok, v, v, zs.at[a, d, k], zr.at[a, d, k], to)
            remote(cond, v, v, xs.at[a, zz], xr.at[a, zz], me.xp)
            onward(a, shard, cond, 0)
    def xstep(a, k):
        alts = ((None, me.z),) if k == 0 else ((me.z - k >= 0, me.z - k), (me.z + k < NZ, me.z + k))
        for cond, zz in alts:
            zz = jnp.clip(zz, 0, NZ - 1)
            shard = 2 * zz + 1 - me.x
            v = view(a, shard, me.y, me.c)
            if cond is None:
                recv(v, v, xr.at[a, zz], me.xp)
            else:
                pl.when(cond)(lambda: recv(v, v, xr.at[a, zz], me.xp))
            onward(a, shard, cond, 1)
    def ystep(a, cond, shard):
        v = view(a, shard, 1 - me.y, me.c)
        def go():
            recv(v, v, yr.at[a, shard], me.yp)
        if cond is None: go()
        else: pl.when(cond)(go)
        remote(cond, v, v, cs.at[a, 1, shard], cr.at[a, 1, shard], me.cp)
    def ysteps(a, k, which):
        if specs[a][0] != "P": return
        if which == "z":
            for cond, zz in ((me.z - k >= 0, me.z - k), (me.z + k < NZ, me.z + k)):
                ystep(a, cond, 2 * jnp.clip(zz, 0, NZ - 1) + me.x)
        elif k == 0:
            ystep(a, None, 2 * me.z + 1 - me.x)
        else:
            for cond, zz in ((me.z - k >= 0, me.z - k), (me.z + k < NZ, me.z + k)):
                ystep(a, cond, 2 * jnp.clip(zz, 0, NZ - 1) + 1 - me.x)
    for k in range(1, NZ + 2):
        for a in order:
            if k < NZ: zstep(a, k)
            if k - 1 < NZ: xstep(a, k - 1)
        for a in order:
            if 1 <= k - 1 < NZ: ysteps(a, k - 1, "z")
            if 0 <= k - 2 < NZ: ysteps(a, k - 2, "x")
    for a in range(n):
        for k in range(1, NZ):
            for cond, zz in ((me.z - k >= 0, me.z - k), (me.z + k < NZ, me.z + k)):
                shard = 2 * jnp.clip(zz, 0, NZ - 1) + me.x
                for w in range(2 if specs[a][0] == "P" else 1):
                    v = view(a, shard, me.y if w == 0 else 1 - me.y, 1 - me.c)
                    pl.when(cond)(lambda: recv(v, v, cr.at[a, w, shard], me.cp))
        for zz in range(NZ):
            shard = 2 * zz + 1 - me.x
            for w in range(2 if specs[a][0] == "P" else 1):
                v = view(a, shard, me.y if w == 0 else 1 - me.y, 1 - me.c)
                recv(v, v, cr.at[a, w, shard], me.cp)
        pltpu.make_async_copy(ins[a], outs[a].at[me.seq], ls.at[a]).wait()
    for cond, cp in sends:
        if cond is None: cp().wait_send()
        else: pl.when(cond)(lambda: cp().wait_send())

def gather_weights(arrays, specs, order, cid):
    n = len(arrays)
    DMA = pltpu.SemaphoreType.DMA
    return pl.pallas_call(
        functools.partial(gather_kernel, specs, order),
        out_shape=[jax.ShapeDtypeStruct((8, *a.shape), a.dtype) for a in arrays],
        in_specs=[pl.BlockSpec(memory_space=pl.ANY)] * n,
        out_specs=[pl.BlockSpec(memory_space=pl.ANY)] * n,
        scratch_shapes=[DMA((n, 2, 3)), DMA((n, 2, 3)), DMA((n, 4)), DMA((n, 4)), DMA((n, 8)), DMA((n, 8)), DMA((n, 2, 8)), DMA((n, 2, 8)), DMA((n,))],
        compiler_params=pltpu.CompilerParams(collective_id=cid, has_side_effects=True),
        name="gather_weights",
    )(*arrays)

class Unit:
    def __init__(self, arr, row, col, flow, axis):
        self.arr, self.row, self.col, self.flow, self.axis = arr, row, col, flow, axis
        self.shape = (row[1], col[1])
        h = list(self.shape); h[axis] //= 2
        self.half = tuple(h)
        q = list(h)
        if flow == "P": q[axis] //= 2
        self.piece = tuple(q)

def rect(unit, ref, part, nparts):
    start = [unit.row[0], unit.col[0]]
    size = list(unit.shape)
    size[unit.axis] //= nparts
    idx = []
    for d in range(2):
        if d == unit.axis:
            off = part * size[d] + start[d]
            idx.append(pl.ds(pl.multiple_of(off, 16 if d == 0 else 128), size[d]))
        else:
            idx.append(pl.ds(start[d], size[d]))
    return ref.at[tuple(idx)]

def reduce_kernel(units, narr, *refs):
    ins, outs = refs[:narr], refs[narr:2 * narr]
    nu = len(units)
    pos = 2 * narr
    A, RC, RY, RX, RZ, RF = [refs[pos + i * nu: pos + (i + 1) * nu] for i in range(6)]
    pos += 6 * nu
    ls, cs, cr, ys, yr, xs, xr, zs, zr, fs, fr, os_ = refs[pos:]
    me = Place()
    greet(me)
    def remote(src, dst, ss, rs, dev):
        return pltpu.make_async_remote_copy(src_ref=src, dst_ref=dst, send_sem=ss, recv_sem=rs, device_id=dev, device_id_type=MESH)
    def shard_at(i):
        zz = lax.rem(me.z + 1 + i // 2, NZ)
        xx = lax.rem(1 - me.x + lax.rem(i, 2), 2)
        return zz, xx, 2 * zz + xx
    def sub(u, ref, y):
        if u.flow == "R":
            return ref
        n = u.piece[u.axis]
        idx = [slice(None)] * 2
        idx[u.axis] = pl.ds(pl.multiple_of(y * n, n), n)
        return ref.at[tuple(idx)]
    def core_copy(k, i):
        u = units[k]; zz, xx, s = shard_at(i)
        return remote(rect(u, ins[u.arr].at[s], 1 - me.c, 2), RC[k].at[s], cs.at[k, s], cr.at[k, s], me.cp)
    def local_copy(k, i):
        u = units[k]; zz, xx, s = shard_at(i)
        return pltpu.make_async_copy(rect(u, ins[u.arr].at[s], me.c, 2), A[k].at[s], ls.at[k, s])
    def y_copy(k, i):
        u = units[k]; zz, xx, s = shard_at(i)
        return remote(sub(u, A[k].at[s], 1 - me.y), RY[k].at[s], ys.at[k, s], yr.at[k, s], me.yp)
    def x_copy(k, zz):
        u = units[k]
        return remote(sub(u, A[k].at[2 * zz + 1 - me.x], me.y), RX[k].at[zz], xs.at[k, zz], xr.at[k, zz], me.xp)
    def z_copy(k, d, zz):
        u = units[k]
        return remote(sub(u, A[k].at[2 * zz + me.x], me.y), RZ[k].at[d, zz], zs.at[k, d, zz], zr.at[k, d, zz], me.up if d == 0 else me.down)
    def add(dst, src):
        dst[...] = dst[...] + src[...]
    def start_core(k):
        def body(i, c):
            core_copy(k, i).start()
            local_copy(k, i).start()
            return c
        lax.fori_loop(0, 8, body, 0)
    def core_stage(k):
        u = units[k]
        def body(i, c):
            zz, xx, s = shard_at(i)
            local_copy(k, i).wait()
            core_copy(k, i).wait_recv()
            add(A[k].at[s], RC[k].at[s])
            if u.flow == "P":
                y_copy(k, i).start()
            else:
                @pl.when(xx != me.x)
                def _(): x_copy(k, zz).start()
            return c
        lax.fori_loop(0, 8, body, 0)
    def y_stage(k):
        u = units[k]
        def body(i, c):
            zz, xx, s = shard_at(i)
            y_copy(k, i).wait_recv()
            add(sub(u, A[k].at[s], me.y), RY[k].at[s])
            @pl.when(xx != me.x)
            def _(): x_copy(k, zz).start()
            return c
        lax.fori_loop(0, 8, body, 0)
    def x_stage(k):
        u = units[k]
        def body(i, c):
            zz = lax.rem(me.z + 1 + i, NZ)
            x_copy(k, zz).wait_recv()
            add(sub(u, A[k].at[2 * zz + me.x], me.y), RX[k].at[zz])
            @pl.when((me.z == 0) & (zz > 0))
            def _(): z_copy(k, 0, zz).start()
            @pl.when((me.z == NZ - 1) & (zz < NZ - 1))
            def _(): z_copy(k, 1, zz).start()
            return c
        lax.fori_loop(0, NZ, body, 0)
    def z_stage(k):
        u = units[k]
        def body(i, c):
            up, down = NZ - 1 - i, i
            @pl.when((up > me.z) & (me.z > 0))
            def _():
                z_copy(k, 0, up).wait_recv()
                add(sub(u, A[k].at[2 * up + me.x], me.y), RZ[k].at[0, up])
                z_copy(k, 0, up).start()
            @pl.when((down < me.z) & (me.z < NZ - 1))
            def _():
                z_copy(k, 1, down).wait_recv()
                add(sub(u, A[k].at[2 * down + me.x], me.y), RZ[k].at[1, down])
                z_copy(k, 1, down).start()
            return c
        lax.fori_loop(0, NZ, body, 0)
    def fin_y(k):
        u = units[k]; mine = sub(u, A[k].at[me.seq], me.y)
        if u.flow == "P":
            dst = rect(u, outs[u.arr], 2 * me.c + me.y, 4)
            return remote(mine, dst, fs.at[k, 0], fr.at[k, 0], me.yp)
        return remote(mine, RF[k], fs.at[k, 0], fr.at[k, 0], me.yp)
    def fin_c(k, w):
        u = units[k]
        if u.flow == "P":
            if w == 0:
                return remote(sub(u, A[k].at[me.seq], me.y), rect(u, outs[u.arr], 2 * me.c + me.y, 4), fs.at[k, 1], fr.at[k, 1], me.cp)
            v = rect(u, outs[u.arr], 2 * me.c + 1 - me.y, 4)
            return remote(v, v, fs.at[k, 2], fr.at[k, 2], me.cp)
        v = rect(u, outs[u.arr], me.c, 2)
        return remote(RF[k], v, fs.at[k, 1], fr.at[k, 1], me.cp)
    def out_copy(k):
        u = units[k]
        if u.flow == "P":
            return pltpu.make_async_copy(sub(u, A[k].at[me.seq], me.y), rect(u, outs[u.arr], 2 * me.c + me.y, 4), os_.at[k])
        return pltpu.make_async_copy(RF[k], rect(u, outs[u.arr], me.c, 2), os_.at[k])
    def own_stage(k):
        u = units[k]
        @pl.when(me.z > 0)
        def _():
            z_copy(k, 0, me.z).wait_recv()
            add(sub(u, A[k].at[me.seq], me.y), RZ[k].at[0, me.z])
        @pl.when(me.z < NZ - 1)
        def _():
            z_copy(k, 1, me.z).wait_recv()
            add(sub(u, A[k].at[me.seq], me.y), RZ[k].at[1, me.z])
        fin_y(k).start()
        if u.flow == "P":
            out_copy(k).start()
            fin_c(k, 0).start()
    def last_stage(k):
        u = units[k]
        fin_y(k).wait_recv()
        if u.flow == "P":
            fin_c(k, 1).start()
        else:
            add(RF[k], A[k].at[me.seq])
            out_copy(k).start()
            fin_c(k, 0).start()
    def end_stage(k):
        u = units[k]
        fin_c(k, 0).wait_recv()
        fin_c(k, 0).wait_send()
        if u.flow == "P":
            fin_c(k, 1).wait_recv()
            fin_c(k, 1).wait_send()
        out_copy(k).wait()
        fin_y(k).wait_send()
        def body(i, c):
            core_copy(k, i).wait_send()
            if u.flow == "P": y_copy(k, i).wait_send()
            return c
        lax.fori_loop(0, 8, body, 0)
        def body(zz, c):
            x_copy(k, zz).wait_send()
            @pl.when((zz > me.z))
            def _(): z_copy(k, 0, zz).wait_send()
            @pl.when((zz < me.z))
            def _(): z_copy(k, 1, zz).wait_send()
            return c
        lax.fori_loop(0, NZ, body, 0)
    for k in range(nu): start_core(k)
    for k in range(nu): core_stage(k)
    Ps = [k for k in range(nu) if units[k].flow == "P"]
    Rs = [k for k in range(nu) if units[k].flow == "R"]
    for i in range(max(len(Ps), len(Rs))):
        if i < len(Ps): y_stage(Ps[i])
        if i < len(Rs): x_stage(Rs[i]);
        if i < len(Rs): z_stage(Rs[i])
    for k in Rs: own_stage(k)
    for k in Ps:
        x_stage(k); z_stage(k)
    for k in Rs: last_stage(k)
    for k in Ps: own_stage(k)
    for k in Ps: last_stage(k)
    for k in range(nu): end_stage(k)

def reduce_weights(arrays, units, cid):
    narr, nu = len(arrays), len(units)
    DMA = pltpu.SemaphoreType.DMA
    bf = jnp.bfloat16
    V = pltpu.VMEM
    scratch = ([V((8, *u.half), bf) for u in units] + [V((8, *u.half), bf) for u in units]
        + [V((8, *u.piece) if u.flow == "P" else (16, 128), bf) for u in units] + [V((4, *u.piece), bf) for u in units]
        + [V((2, 4, *u.piece), bf) for u in units] + [V(u.piece if u.flow == "R" else (16, 128), bf) for u in units]
        + [DMA((nu, 8))] * 5 + [DMA((nu, 4))] * 2 + [DMA((nu, 2, 4))] * 2 + [DMA((nu, 3))] * 2 + [DMA((nu,))])
    return pl.pallas_call(
        functools.partial(reduce_kernel, units, narr),
        out_shape=[jax.ShapeDtypeStruct(a.shape[1:], a.dtype) for a in arrays],
        in_specs=[pl.BlockSpec(memory_space=pl.ANY)] * narr,
        out_specs=[pl.BlockSpec(memory_space=pl.ANY)] * narr,
        scratch_shapes=scratch,
        compiler_params=pltpu.CompilerParams(collective_id=cid, has_side_effects=True, vmem_limit_bytes=58 << 20),
        name="reduce_weights",
    )(*arrays)

def gather_rows_kernel(src, out, zs, zr, xs, xr, ls):
    me = Place()
    greet(me)
    rows = src.shape[0]
    def remote(s, b, ss, rs, dev):
        v = out.at[s, b]
        return pltpu.make_async_remote_copy(src_ref=v, dst_ref=v, send_sem=ss, recv_sem=rs, device_id=dev, device_id_type=MESH)
    def first(b, ss, rs, dev):
        return pltpu.make_async_remote_copy(src_ref=src.at[b], dst_ref=out.at[me.seq, b], send_sem=ss, recv_sem=rs, device_id=dev, device_id_type=MESH)
    sends = []
    def start(cond, mk):
        pl.when(cond)(lambda: mk().start())
        sends.append((cond, mk))
    for b in range(rows):
        start(me.z < NZ - 1, functools.partial(first, b, zs.at[b, 0, 0], zr.at[b, 0, 0], me.up))
        start(me.z > 0, functools.partial(first, b, zs.at[b, 1, 0], zr.at[b, 1, 0], me.down))
        start(me.z >= 0, functools.partial(first, b, xs.at[b, me.z], xr.at[b, me.z], me.xp))
    for b in range(rows):
        pltpu.make_async_copy(src.at[b], out.at[me.seq, b], ls.at[b]).start()
    for k in range(1, NZ):
        for b in range(rows):
            for d, (cond, zz, fwd, to) in enumerate((
                (me.z - k >= 0, me.z - k, me.z < NZ - 1, me.up),
                (me.z + k < NZ, me.z + k, me.z > 0, me.down))):
                zz = jnp.clip(zz, 0, NZ - 1)
                s = 2 * zz + me.x
                pl.when(cond)(lambda: remote(s, b, zr.at[b, d, k - 1], zr.at[b, d, k - 1], to).wait_recv())
                if k < NZ - 1:
                    start(cond & fwd, functools.partial(remote, s, b, zs.at[b, d, k], zr.at[b, d, k], to))
                start(cond, functools.partial(remote, s, b, xs.at[b, zz], xr.at[b, zz], me.xp))
    for b in range(rows):
        for zz in range(NZ):
            remote(2 * zz + 1 - me.x, b, xs.at[b, zz], xr.at[b, zz], me.xp).wait_recv()
        pltpu.make_async_copy(src.at[b], out.at[me.seq, b], ls.at[b]).wait()
    for cond, mk in sends:
        pl.when(cond)(lambda: mk().wait_send())

def gather_rows(a, cid):
    DMA = pltpu.SemaphoreType.DMA
    r = a.shape[0]
    return pl.pallas_call(
        gather_rows_kernel,
        out_shape=jax.ShapeDtypeStruct((8, *a.shape), a.dtype),
        in_specs=[pl.BlockSpec(memory_space=pl.ANY)],
        out_specs=pl.BlockSpec(memory_space=pl.ANY),
        scratch_shapes=[DMA((r, 2, 3)), DMA((r, 2, 3)), DMA((r, 4)), DMA((r, 4)), DMA((r,))],
        compiler_params=pltpu.CompilerParams(collective_id=cid, has_side_effects=True),
        name="gather_rows",
    )(a)

def reduce_rows_kernel(src, out, A, RX, RZ, xs, xr, zs, zr, ls):
    me = Place()
    greet(me)
    rows = src.shape[1]
    def remote(s, d, ss, rs, dev):
        return pltpu.make_async_remote_copy(src_ref=s, dst_ref=d, send_sem=ss, recv_sem=rs, device_id=dev, device_id_type=MESH)
    def local(b, zz):
        return pltpu.make_async_copy(src.at[2 * zz + me.x, b], A.at[b, zz], ls.at[b, zz])
    def x_copy(b, zz):
        return remote(src.at[2 * zz + 1 - me.x, b], RX.at[b, zz], xs.at[b, zz], xr.at[b, zz], me.xp)
    def z_copy(b, d, zz):
        return remote(A.at[b, zz], RZ.at[b, d, zz], zs.at[b, d, zz], zr.at[b, d, zz], me.up if d == 0 else me.down)
    def add(dst, more):
        dst[...] = dst[...] + more[...]
    def turn(i):
        return lax.rem(me.z + 1 + i, NZ)
    def begin(i, c):
        for b in range(rows):
            x_copy(b, turn(i)).start()
            local(b, turn(i)).start()
        return c
    lax.fori_loop(0, NZ, begin, 0)
    for b in range(rows):
        def arrive(i, c):
            zz = turn(i)
            local(b, zz).wait()
            x_copy(b, zz).wait_recv()
            add(A.at[b, zz], RX.at[b, zz])
            pl.when((me.z == 0) & (zz > 0))(lambda: z_copy(b, 0, zz).start())
            pl.when((me.z == NZ - 1) & (zz < NZ - 1))(lambda: z_copy(b, 1, zz).start())
            return c
        lax.fori_loop(0, NZ, arrive, 0)
    for b in range(rows):
        def pass_on(i, c):
            up, down = NZ - 1 - i, i
            @pl.when((up > me.z) & (me.z > 0))
            def _():
                z_copy(b, 0, up).wait_recv()
                add(A.at[b, up], RZ.at[b, 0, up])
                z_copy(b, 0, up).start()
            @pl.when((down < me.z) & (me.z < NZ - 1))
            def _():
                z_copy(b, 1, down).wait_recv()
                add(A.at[b, down], RZ.at[b, 1, down])
                z_copy(b, 1, down).start()
            return c
        lax.fori_loop(0, NZ, pass_on, 0)
    for b in range(rows):
        @pl.when(me.z > 0)
        def _():
            z_copy(b, 0, me.z).wait_recv()
            add(A.at[b, me.z], RZ.at[b, 0, me.z])
        @pl.when(me.z < NZ - 1)
        def _():
            z_copy(b, 1, me.z).wait_recv()
            add(A.at[b, me.z], RZ.at[b, 1, me.z])
        out[b] = A[b, me.z]
        def sent(zz, c):
            x_copy(b, zz).wait_send()
            pl.when(zz > me.z)(lambda: z_copy(b, 0, zz).wait_send())
            pl.when(zz < me.z)(lambda: z_copy(b, 1, zz).wait_send())
            return c
        lax.fori_loop(0, NZ, sent, 0)

def reduce_rows(a, cid):
    DMA = pltpu.SemaphoreType.DMA
    shape = a.shape[1:]
    r = shape[0]
    V = pltpu.VMEM
    return pl.pallas_call(
        reduce_rows_kernel,
        out_shape=jax.ShapeDtypeStruct(shape, a.dtype),
        in_specs=[pl.BlockSpec(memory_space=pl.ANY)],
        out_specs=pl.BlockSpec(memory_space=pltpu.VMEM),
        scratch_shapes=[V((r, 4, *shape[1:]), a.dtype), V((r, 4, *shape[1:]), a.dtype), V((r, 2, 4, *shape[1:]), a.dtype),
                        DMA((r, 4)), DMA((r, 4)), DMA((r, 2, 4)), DMA((r, 2, 4)), DMA((r, 4))],
        compiler_params=pltpu.CompilerParams(collective_id=cid, has_side_effects=True, vmem_limit_bytes=32 << 20),
        name="reduce_rows",
    )(a)
F32, BF16 = jnp.float32, jnp.bfloat16
NEG = -1e30

def nn(a, b):
    return lax.dot_general(a, b, (((1,), (0,)), ((), ())), preferred_element_type=F32)

def nt(a, b):
    return lax.dot_general(a, b, (((1,), (1,)), ((), ())), preferred_element_type=F32)

def expand(heads, dims, base):
    parts = []
    for h in range(2):
        parts.append((heads[base + h:base + h + 1] * dims[0] + heads[base + 2 + h:base + 3 + h] * dims[1]) * 0.5)
    return jnp.concatenate(parts, 0)

def queries(qh, qr):
    parts = []
    for h in range(2):
        total = qh[h:h + 1] * qr[0:64]
        for r in range(1, 6):
            total = total + qh[2 * r + h:2 * r + h + 1] * qr[64 * r:64 * r + 64]
        parts.append(total)
    return jnp.concatenate(parts, 0) / 6.0

def lanes_below(shape, n):
    return lax.broadcasted_iota(jnp.int32, shape, 1) < n

def stack_heads(part):
    first = lanes_below(part.shape, 64)
    zero = jnp.zeros_like(part)
    return jnp.concatenate([jnp.where(first, part, zero), jnp.where(first, zero, part)], 0)

def unstack_heads(part):
    n = part.shape[0] // 2
    return jnp.where(lanes_below((n, 128), 64), part[:n], part[n:])

def causal_bias(n2, span):
    row = lax.broadcasted_iota(jnp.int32, (n2, span), 0) % span
    col = lax.broadcasted_iota(jnp.int32, (n2, span), 1)
    return jnp.where(col <= row, 0.0, NEG)

def pair_factors(heads, dims, cond, base, at):
    hl, hs = heads
    dl, ds = dims
    low = expand(hl, (dl[at:at + 64].astype(F32), dl[at + 64:at + 128].astype(F32)), base).astype(BF16)
    sel = expand(hs, (ds[at:at + 64].astype(F32), ds[at + 64:at + 128].astype(F32)), base)
    left = jnp.where(cond > 0.5, sel, 0.0).astype(BF16)
    right = jnp.where(cond > 0.5, 0.0, sel).astype(BF16)
    return low, jnp.concatenate([left, right], 0)

def attend_kernel(span, chunk, qh_ref, qr_ref, hl_ref, hs_ref, dl_ref, ds_ref, cond_ref, bl_ref, bs_ref, o_ref, lse_ref, s1, s2):
    p = pl.program_id(1)
    n2 = 2 * span
    nk = dl_ref.shape[-1]
    qt = queries(qh_ref[0, 0], qr_ref[0])
    q = (qt.T.astype(BF16) * BF16(0.125)) if False else (qt.astype(BF16).astype(F32).T * 0.125).astype(BF16)
    qlo, qhi = stack_heads(q[:span]), stack_heads(q[span:])
    qboth = jnp.concatenate([qlo, qhi], 1)
    heads = (hl_ref[0, 0], hs_ref[0, 0])
    dims = (dl_ref[0], ds_ref[0])
    cond = cond_ref[...]
    klo, ksel = pair_factors(heads, dims, cond, 0, 0)
    vlo, vsel = pair_factors(heads, dims, cond, 4, 128)
    tri = causal_bias(n2, span)
    width = min(128, chunk)
    mlo = jnp.full((n2, width), NEG, F32)
    mhi = jnp.full((n2, width), NEG, F32)
    s3 = nn(qlo, klo[:, :span]) + bl_ref[0][:, :span] + tri
    m3 = jnp.max(s3, -1, keepdims=True)
    for c in range(0, nk, chunk):
        sl = slice(c, c + chunk)
        a = nn(qhi, klo[:, sl]) + bl_ref[0][:, sl]
        s1[:, sl] = a
        b = nn(qboth, ksel[:, sl]) + bs_ref[0][:, sl]
        if c == 0:
            b = jnp.concatenate([b[:, :span] + tri, b[:, span:]], 1)
        s2[:, sl] = b
        for i in range(0, chunk, width):
            on = cond[:, c + i:c + i + width] > 0.5
            ai, bi = a[:, i:i + width], b[:, i:i + width]
            mlo = jnp.maximum(mlo, jnp.where(on, bi, NEG))
            mhi = jnp.maximum(mhi, jnp.maximum(ai, jnp.where(on, NEG, bi)))
    mlo = jnp.maximum(jnp.max(mlo, -1, keepdims=True), m3)
    mhi = jnp.max(mhi, -1, keepdims=True)
    e3 = jnp.exp(s3 - mlo)
    tlo = jnp.zeros((n2, width), F32)
    thi = jnp.zeros((n2, width), F32)
    o3 = nt(e3.astype(BF16), vlo[:, :span])
    o1 = jnp.zeros((n2, 128), F32)
    o2 = jnp.zeros((n2, 256), F32)
    for c in range(0, nk, chunk):
        sl = slice(c, c + chunk)
        on = cond[:, sl] > 0.5
        a = jnp.exp(s1[:, sl] - mhi)
        b = jnp.exp(s2[:, sl] - jnp.where(on, mlo, mhi))
        blo = jnp.where(on, b, 0.0)
        bhi = a + jnp.where(on, 0.0, b)
        for i in range(0, chunk, width):
            tlo = tlo + blo[:, i:i + width]
            thi = thi + bhi[:, i:i + width]
        o1 = o1 + nt(a.astype(BF16), vlo[:, sl])
        o2 = o2 + nt(b.astype(BF16), vsel[:, sl])
    llo = jnp.sum(tlo, -1, keepdims=True) + jnp.sum(e3, -1, keepdims=True)
    lhi = jnp.sum(thi, -1, keepdims=True)
    olo = unstack_heads((o2[:, :128] + o3) / llo)
    ohi = unstack_heads((o2[:, 128:] + o1) / lhi)
    o_ref[0] = jnp.concatenate([olo, ohi], 0).astype(BF16)
    lane = lax.broadcasted_iota(jnp.int32, (span, 128), 1)
    tlo = mlo + jnp.log(llo)
    thi = mhi + jnp.log(lhi)
    old = jnp.where(p == 0, 0.0, lse_ref[0])
    new = []
    for k, t in enumerate((tlo, thi)):
        part = old[k * span:(k + 1) * span]
        part = jnp.where(lane == 2 * p, t[:span], part)
        new.append(jnp.where(lane == 2 * p + 1, t[span:], part))
    lse_ref[0] = jnp.concatenate(new, 0)

def attend(qh, qr, hl, hs, dl, ds, cond, bl, bs):
    rows, pairs, _, nq = qh.shape
    nk = dl.shape[-1]
    span = nq // 2
    chunk = min(512, nk)
    full = lambda *s: pl.BlockSpec((1, *s), lambda b, p: (b, *([0] * len(s))))
    pairb = lambda *s: pl.BlockSpec((1, 1, *s), lambda b, p: (b, p, *([0] * len(s))))
    return pl.pallas_call(
        functools.partial(attend_kernel, span, chunk),
        grid=(rows, pairs),
        out_shape=[jax.ShapeDtypeStruct((rows, nq, pairs * 128), BF16), jax.ShapeDtypeStruct((rows, nq, 128), F32)],
        in_specs=[pairb(12, nq), full(384, nq), pairb(8, nk), pairb(8, nk), full(256, nk), full(256, nk),
                  pl.BlockSpec((1, nk), lambda b, p: (0, 0)), full(1, nk), full(1, nk)],
        out_specs=[pl.BlockSpec((1, nq, 128), lambda b, p: (b, 0, p)), full(nq, 128)],
        scratch_shapes=[pltpu.VMEM((nq, nk), F32), pltpu.VMEM((nq, nk), F32)],
        compiler_params=pltpu.CompilerParams(vmem_limit_bytes=56 << 20),
        name="attend",
    )(qh, qr, hl, hs, dl, ds, cond, bl, bs)

def attend_back_kernel(span, chunk, qh_ref, qr_ref, hl_ref, hs_ref, dl_ref, ds_ref, cond_ref, bl_ref, bs_ref, lse_ref, o_ref, g_ref,
                       dqh_ref, dqr_ref, dhl_ref, dhs_ref, ddl_ref, dds_ref):
    p = pl.program_id(1)
    n2 = 2 * span
    nk = dl_ref.shape[-1]
    qh, qr = qh_ref[0, 0], qr_ref[0]
    qt = (queries(qh, qr).astype(BF16).astype(F32)) * 0.125
    q = qt.T.astype(BF16)
    qlo, qhi = stack_heads(q[:span]), stack_heads(q[span:])
    qboth = jnp.concatenate([qlo, qhi], 1)
    g = g_ref[0]
    glo, ghi = stack_heads(g[:span]), stack_heads(g[span:])
    gboth = jnp.concatenate([glo, ghi], 1)
    gt = g.astype(F32).T
    first = lax.broadcasted_iota(jnp.int32, (128, span), 0) < 64
    def stack_lanes(part):
        return jnp.concatenate([jnp.where(first, part, 0.0), jnp.where(first, 0.0, part)], 1).astype(BF16)
    qtlo, qthi = stack_lanes(qt[:, :span]), stack_lanes(qt[:, span:])
    gtlo, gthi = stack_lanes(gt[:, :span]), stack_lanes(gt[:, span:])
    qtboth = jnp.concatenate([qtlo, qthi], 0)
    gtboth = jnp.concatenate([gtlo, gthi], 0)
    prod = g.astype(F32) * o_ref[0].astype(F32)
    flane = lanes_below((n2, 128), 64)
    d0 = jnp.sum(jnp.where(flane, prod, 0.0), -1, keepdims=True)
    d1 = jnp.sum(jnp.where(flane, 0.0, prod), -1, keepdims=True)
    lane = lax.broadcasted_iota(jnp.int32, (n2, 128), 1)
    lse = lse_ref[0]
    l0 = jnp.sum(jnp.where(lane == 2 * p, lse, 0.0), -1, keepdims=True)
    l1 = jnp.sum(jnp.where(lane == 2 * p + 1, lse, 0.0), -1, keepdims=True)
    dello, delhi = jnp.concatenate([d0[:span], d1[:span]], 0), jnp.concatenate([d0[span:], d1[span:]], 0)
    lselo, lsehi = jnp.concatenate([l0[:span], l1[:span]], 0), jnp.concatenate([l0[span:], l1[span:]], 0)
    heads = (hl_ref[0, 0], hs_ref[0, 0])
    dims = (dl_ref[0], ds_ref[0])
    cond = cond_ref[...]
    klo, ksel = pair_factors(heads, dims, cond, 0, 0)
    vlo, vsel = pair_factors(heads, dims, cond, 4, 128)
    tri = causal_bias(n2, span)

    @pl.when(p == 0)
    def _():
        dqr_ref[...] = jnp.zeros_like(dqr_ref)
        ddl_ref[...] = jnp.zeros_like(ddl_ref)
        dds_ref[...] = jnp.zeros_like(dds_ref)

    def put(dkt, h_ref, d_ref, hd_ref, dd_ref, base, at, sl):
        for r in range(2):
            dim = d_ref[0, at + 64 * r:at + 64 * r + 64, sl].astype(F32)
            total = None
            for h in range(2):
                part = dkt[64 * h:64 * h + 64]
                j = base + 2 * r + h
                hd_ref[0, 0, j:j + 1, sl] = jnp.sum(part * dim, 0, keepdims=True) * 0.5
                term = part * h_ref[0, 0, j:j + 1, sl]
                total = term if total is None else total + term
            dd_ref[0, at + 64 * r:at + 64 * r + 64, sl] += total * 0.5

    s3 = nn(qlo, klo[:, :span]) + bl_ref[0][:, :span] + tri
    p3 = jnp.exp(s3 - lselo)
    dp3 = nn(glo, vlo[:, :span])
    ds3 = (p3 * (dp3 - dello)).astype(BF16)
    p3 = p3.astype(BF16)
    dq3 = nt(ds3, klo[:, :span])
    dk3 = nn(qtlo, ds3)
    dv3 = nn(gtlo, p3)
    dq1 = jnp.zeros((n2, 128), F32)
    dq2 = jnp.zeros((n2, 256), F32)
    for c in range(0, nk, chunk):
        sl = slice(c, c + chunk)
        pa = jnp.exp(nn(qhi, klo[:, sl]) + bl_ref[0][:, sl] - lsehi)
        dpa = nn(ghi, vlo[:, sl])
        dsa = (pa * (dpa - delhi)).astype(BF16)
        pa = pa.astype(BF16)
        dq1 = dq1 + nt(dsa, klo[:, sl])
        dk = nn(qthi, dsa)
        dv = nn(gthi, pa)
        if c == 0:
            dk = jnp.concatenate([dk[:, :span] + dk3, dk[:, span:]], 1)
            dv = jnp.concatenate([dv[:, :span] + dv3, dv[:, span:]], 1)
        put(dk, hl_ref, dl_ref, dhl_ref, ddl_ref, 0, 0, sl)
        put(dv, hl_ref, dl_ref, dhl_ref, ddl_ref, 4, 128, sl)
    for c in range(0, nk, chunk):
        sl = slice(c, c + chunk)
        on = cond[:, sl] > 0.5
        s = nn(qboth, ksel[:, sl]) + bs_ref[0][:, sl]
        if c == 0:
            s = jnp.concatenate([s[:, :span] + tri, s[:, span:]], 1)
        pb = jnp.exp(s - jnp.where(on, lselo, lsehi))
        dpb = nn(gboth, vsel[:, sl])
        dsb = (pb * (dpb - jnp.where(on, dello, delhi))).astype(BF16)
        pb = pb.astype(BF16)
        dq2 = dq2 + nt(dsb, ksel[:, sl])
        dk = nn(qtboth, dsb)
        dv = nn(gtboth, pb)
        dk = jnp.where(on, dk[:128], dk[128:])
        dv = jnp.where(on, dv[:128], dv[128:])
        put(dk, hs_ref, ds_ref, dhs_ref, dds_ref, 0, 0, sl)
        put(dv, hs_ref, ds_ref, dhs_ref, dds_ref, 4, 128, sl)
    dqlo = unstack_heads(dq2[:, :128] + dq3)
    dqhi = unstack_heads(dq2[:, 128:] + dq1)
    dqt = (jnp.concatenate([dqlo, dqhi], 0) * (0.125 / 6.0)).T
    for r in range(6):
        total = None
        for h in range(2):
            part = dqt[64 * h:64 * h + 64]
            j = 2 * r + h
            dqh_ref[0, 0, j:j + 1, :] = jnp.sum(part * qr[64 * r:64 * r + 64], 0, keepdims=True)
            term = part * qh[j:j + 1]
            total = term if total is None else total + term
        dqr_ref[0, 64 * r:64 * r + 64, :] += total

def attend_back(qh, qr, hl, hs, dl, ds, cond, bl, bs, lse, o, g):
    rows, pairs, _, nq = qh.shape
    nk = dl.shape[-1]
    span = nq // 2
    chunk = min(512, nk)
    full = lambda *s: pl.BlockSpec((1, *s), lambda b, p: (b, *([0] * len(s))))
    pairb = lambda *s: pl.BlockSpec((1, 1, *s), lambda b, p: (b, p, *([0] * len(s))))
    tok = pl.BlockSpec((1, nq, 128), lambda b, p: (b, 0, p))
    sd = jax.ShapeDtypeStruct
    return pl.pallas_call(
        functools.partial(attend_back_kernel, span, chunk),
        grid=(rows, pairs),
        out_shape=[sd((rows, pairs, 12, nq), F32), sd((rows, 384, nq), F32), sd((rows, pairs, 8, nk), F32), sd((rows, pairs, 8, nk), F32),
                   sd((rows, 256, nk), F32), sd((rows, 256, nk), F32)],
        in_specs=[pairb(12, nq), full(384, nq), pairb(8, nk), pairb(8, nk), full(256, nk), full(256, nk),
                  pl.BlockSpec((1, nk), lambda b, p: (0, 0)), full(1, nk), full(1, nk), full(nq, 128), tok, tok],
        out_specs=[pairb(12, nq), full(384, nq), pairb(8, nk), pairb(8, nk), full(256, nk), full(256, nk)],
        compiler_params=pltpu.CompilerParams(vmem_limit_bytes=56 << 20),
        name="attend_back",
    )(qh, qr, hl, hs, dl, ds, cond, bl, bs, lse, o, g)

HEADS, HDIM, QRANK, KVRANK = 16, 64, 6, 2
PAIRS = HEADS // 2
EPSILON = 1e-06


def rms_forward(values, gain):
    scale = lax.rsqrt(jnp.mean(values * values, -1, keepdims=True) + EPSILON)
    unit = values * scale
    return (unit * gain, unit, scale)


def rms_backward(grad_out, unit, scale, gain):
    scaled = grad_out * gain
    grad_in = scale * (scaled - unit * jnp.mean(scaled * unit, -1, keepdims=True))
    return (grad_in, jnp.sum(grad_out * unit, 0))


def rotation(positions):
    half = HDIM // 2
    index = jnp.arange(half).astype(F32)
    inverse = jnp.exp(index * (-math.log(10000.0) / half))
    angles = inverse[:, None] * positions.astype(F32)[None, :]
    return (jnp.cos(angles), jnp.sin(angles))


def rotate(u, cosine, sine):
    rows, depth, slots = u.shape
    v = u.reshape(rows, depth // HDIM, HDIM, slots)
    a, b = v[:, :, :HDIM // 2], v[:, :, HDIM // 2:]
    return jnp.concatenate([a * cosine - b * sine, b * cosine + a * sine], 2).reshape(u.shape)


def dot(a, b, ca, cb):
    return lax.dot_general(a, b, ((ca, cb), ((), ())), preferred_element_type=F32)


def pair_rows(a, ranks):
    rows, _, n = a.shape
    return a.reshape(rows, ranks, PAIRS, 2, n).transpose(0, 2, 1, 3, 4).reshape(rows, PAIRS, ranks * 2, n)


def unpair_rows(a, ranks):
    rows, _, _, n = a.shape
    return a.reshape(rows, PAIRS, ranks, 2, n).transpose(0, 2, 1, 3, 4).reshape(rows, ranks * HEADS, n)


GATHER_SPECS = [("R", 0, 128), ("P", 0, 128), ("P", 0, 128), ("R", 0, 128), ("P", 1, 1024)]
REDUCE_UNITS = [
    Unit(4, (0, 176), (0, 1024), "P", 1), Unit(3, (0, 128), (0, 1408), "R", 0),
    Unit(4, (176, 176), (0, 1024), "P", 1), Unit(3, (0, 128), (1408, 1408), "R", 0),
    Unit(2, (0, 128), (0, 1408), "P", 0), Unit(1, (0, 128), (0, 1024), "R", 0),
    Unit(2, (0, 128), (1408, 1408), "P", 0), Unit(0, (0, 128), (0, 896), "R", 0)]


def gather_all(near, arrays):
    if near:
        return gather_weights(arrays, GATHER_SPECS, [0, 2, 4, 3, 1], 0)
    return [lax.all_gather(a, "seq", axis=0) for a in arrays]


def reduce_all(near, arrays):
    if near:
        return reduce_weights(arrays, REDUCE_UNITS, 1)
    out = []
    for a in arrays:
        own = lax.psum_scatter(a.astype(F32), "seq", scatter_dimension=0, tiled=True)[0]
        out.append(lax.psum(own.astype(BF16), "batch"))
    return out


def per_device(near, tokens, cotangent, lengths, span_order, attn_gain, query_heads, query_dims, key_heads, key_dims,
               value_heads, value_dims, out_proj, ffn_gain, gate_proj, up_proj, down_proj):
    rows, slots, width = tokens.shape
    span = slots // 2
    count = rows * slots
    nseq = span_order.shape[0]
    nk = nseq * span
    me = lax.axis_index("seq")
    small = jnp.concatenate([query_heads, query_dims, key_dims, value_dims, key_heads, value_heads, attn_gain[:, None], ffn_gain[:, None]], 1)
    small = jnp.pad(small, ((0, 0), (0, 896 - small.shape[1])))
    parts = gather_all(near, [small, out_proj, gate_proj, up_proj, down_proj])
    small, w_out, w_gate, w_up, w_down = [p.reshape(-1, p.shape[-1]) for p in parts]
    w_qkv = small[:, :800]
    gain_one = small[:, 800].astype(F32)
    gain_two = small[:, 801].astype(F32)

    offsets = jnp.arange(span, dtype=jnp.int32)
    spans = jnp.concatenate([span_order, span_order], 0)
    spans = lax.dynamic_slice_in_dim(spans, me, nseq, 0)
    local_pos = (spans[0][:, None] * span + offsets[None, :]).reshape(-1)
    cosine, sine = rotation(local_pos)
    chosen = spans[:, 0] < spans[0, 0]
    low_pos = (spans[:, 0][:, None] * span + offsets[None, :]).reshape(1, nk)
    sel_pos = (jnp.where(chosen, spans[:, 0], spans[:, 1])[:, None] * span + offsets[None, :]).reshape(1, nk)
    cond = jnp.repeat(chosen.astype(F32), span).reshape(1, nk)
    low_bias = jnp.where(low_pos < lengths[:, None], 0.0, NEG)[:, None, :]
    sel_bias = jnp.where(sel_pos < lengths[:, None], 0.0, NEG)[:, None, :]

    flat = tokens.reshape(count, width).astype(F32)
    normed_full, unit_one, scale_one = rms_forward(flat, gain_one)
    normed = normed_full.astype(BF16)
    by_row = normed.reshape(rows, slots, width)
    factors = jnp.stack([dot(w_qkv, by_row[b], (0,), (1,)) for b in range(rows)])
    qh = factors[:, :96]
    qr = rotate(factors[:, 96:480], cosine, sine)
    own = jnp.concatenate([rotate(factors[:, 480:608], cosine, sine), factors[:, 608:800]], 1).astype(BF16)
    shared = gather_rows(own, 2) if near else lax.all_gather(own, "seq", axis=0)
    shared = lax.dynamic_slice_in_dim(jnp.concatenate([shared, shared], 0), me, nseq, 0)
    low, high = shared[..., :span], shared[..., span:]
    sel = jnp.where(chosen[:, None, None, None], low, high)
    low = low.transpose(1, 2, 0, 3).reshape(rows, 320, nk)
    sel = sel.transpose(1, 2, 0, 3).reshape(rows, 320, nk)
    att = (pair_rows(qh, QRANK), qr, pair_rows(low[:, 256:].astype(F32), 4), pair_rows(sel[:, 256:].astype(F32), 4),
           low[:, :256], sel[:, :256], cond, low_bias, sel_bias)
    heads_out, lse = attend(*att)
    heads_flat = heads_out.reshape(count, width)

    resid = flat + dot(heads_flat, w_out, (1,), (0,))
    normed_two_full, unit_two, scale_two = rms_forward(resid, gain_two)
    normed_two = normed_two_full.astype(BF16)
    gate = dot(normed_two, w_gate, (1,), (0,))
    up_part = dot(normed_two, w_up, (1,), (0,))
    sigma = jax.nn.sigmoid(gate)
    hidden = (gate * sigma * up_part).astype(BF16)
    output = (resid + dot(hidden, w_down, (1,), (0,))).astype(BF16).reshape(rows, slots, width)

    grad_out = cotangent.reshape(count, width)
    down_grad = dot(hidden, grad_out, (0,), (0,)).astype(BF16)
    d_hidden = dot(grad_out, w_down, (1,), (1,))
    d_gate = (d_hidden * up_part * sigma * (1.0 + gate * (1.0 - sigma))).astype(BF16)
    d_up = (d_hidden * gate * sigma).astype(BF16)
    gate_grad = dot(normed_two, d_gate, (0,), (0,)).astype(BF16)
    up_grad = dot(normed_two, d_up, (0,), (0,)).astype(BF16)
    d_normed_two = dot(d_gate, w_gate, (1,), (1,)) + dot(d_up, w_up, (1,), (1,))
    d_mid, gain_two_grad = rms_backward(d_normed_two, unit_two, scale_two, gain_two)
    d_resid = grad_out.astype(F32) + d_mid
    d_attn = d_resid.astype(BF16)
    out_grad = dot(heads_flat, d_attn, (0,), (0,)).astype(BF16)
    d_heads = dot(d_attn, w_out, (1,), (1,)).astype(BF16).reshape(rows, slots, width)

    dqh, dqr, dhl, dhs, ddl, dds = attend_back(*att, lse, heads_out, d_heads)
    from_low = jnp.concatenate([ddl, unpair_rows(dhl, 4)], 1).reshape(rows, 320, nseq, span)
    from_sel = jnp.concatenate([dds, unpair_rows(dhs, 4)], 1).reshape(rows, 320, nseq, span)
    pick = chosen[None, None, :, None]
    both = jnp.concatenate([from_low + jnp.where(pick, from_sel, 0.0), jnp.where(pick, 0.0, from_sel)], -1)
    both = both.astype(BF16) if near else both
    both = both.transpose(2, 0, 1, 3)
    both = lax.dynamic_slice_in_dim(jnp.concatenate([both, both], 0), lax.rem(nseq - me, nseq), nseq, 0)
    mine = (reduce_rows(both, 3) if near else lax.psum_scatter(both, "seq", scatter_dimension=0, tiled=True)[0]).astype(F32)
    turned = jnp.concatenate([unpair_rows(dqh, QRANK), rotate(dqr, cosine, -sine), rotate(mine[:, :128], cosine, -sine), mine[:, 128:]], 1).astype(BF16)
    small_grad = dot(by_row, turned, (0, 1), (0, 2))
    d_normed = dot(turned, w_qkv, (1,), (1,)).reshape(count, width)
    d_first, gain_one_grad = rms_backward(d_normed, unit_one, scale_one, gain_one)
    input_grad = (d_resid + d_first).reshape(rows, slots, width)
    small_grad = jnp.concatenate([small_grad, gain_one_grad[:, None], gain_two_grad[:, None], jnp.zeros((width, 94), F32)], 1).astype(BF16)

    grads = [g.reshape(nseq, -1, g.shape[-1]) for g in (small_grad, out_grad, gate_grad, up_grad, down_grad)]
    small_sum, out_sum, gate_sum, up_sum, down_sum = [g.astype(F32) for g in reduce_all(near, grads)]
    return (output, input_grad, small_sum[:, 800], small_sum[:, :96], small_sum[:, 96:480], small_sum[:, 736:768], small_sum[:, 480:608],
            small_sum[:, 768:800], small_sum[:, 608:736], out_sum, small_sum[:, 801], gate_sum, up_sum, down_sum)


def solution(mesh):
    near = mesh.shape["seq"] == 8 and mesh.shape["batch"] == 4
    by_slot = P("batch", "seq", None)
    line, table = P("seq"), P("seq", None)
    return jax.shard_map(
        functools.partial(per_device, near),
        mesh=mesh,
        in_specs=(by_slot, by_slot, P("batch"), P(), line, *([table] * 7), line, *([table] * 3)),
        out_specs=(by_slot, by_slot, line, *([table] * 7), line, *([table] * 3)),
        check_vma=False,
    )
```

time: 2530 us -> 587 us (0.23)
  waiting for transfers between devices: 1290 us -> 0 us
  matrix products: 539 us -> 75.2 us
  Pallas kernels: 0 us -> 413 us
  blocking collectives: 300 us -> 0 us
  local copies, waits for them, and re-layouts: 206 us -> 57.6 us
  other arithmetic: 135 us -> 30.7 us
  loops' own time: 30.5 us -> 0 us
    reduce_scatter x14 -> x0, waiting for transfers between devices: 1210 us -> none  [the longest x1 194 us: per_device(): lax.psum_scatter(gate_grad, 'seq', scatter_dimension=0, tiled=True)]
    dot_general x63 -> x16, matrix products: 539 us -> 75.2 us  [dot(): lax.dot_general(a, b, ((ca, cb), ((), ())), preferred_element_type=F32)]
    pallas_call x0 -> x6, Pallas kernels: none -> 413 us  [the longest x1 143 us: reduce_weights(): pl.pallas_call(functools.partial(reduce_kernel, units, narr), out_shape=[...]
    all_gather x10 -> x0, blocking collectives: 280 us -> none  [the longest x1 35.7 us: per_device(): lax.all_gather(query_dims, 'seq', axis=0, tiled=True)]
    convert_element_type x34 -> x10, other arithmetic: 93.4 us -> 8.85 us  [the longest x5 5.54 us: per_device(): g.astype(F32)]
    psum x2 -> x0, waiting for transfers between devices: 77.2 us -> none  [the longest x1 55.8 us: per_device(): lax.psum(summed[2].astype(jnp.bfloat16), 'batch').astype(jnp.float32)]
    dot_general x9 -> x0, local copies, waits for them, and re-layouts: 59.8 us -> none  [the longest x4 51.5 us: expand_factors(): jnp.einsum('krh,krd->khd', head_full, dims_full, precision=HIGH) / KVRANK]
    reduce_sum x2 -> x0, other arithmetic: 30.5 us -> none  [attend_row(): jnp.sum(jnp.exp(scores - peak), -1, keepdims=True)]
  transfers between devices with their start and end apart: 22 -> 0, of which waited for: 16 -> 0; matrix products, arithmetic and copies ran while one was open for 12% -> 0% of each run, Pallas kernels for 0% -> 0%
where the time goes in v1:
time: 587 us; the launch traced here: 578 us
  Pallas kernels  413 us (70%)
  matrix products  75.2 us (13%)
  local copies, waits for them, and re-layouts  57.6 us (10%)
  other arithmetic  30.7 us (5%)
    pallas_call x1, Pallas kernels, reduce_weights(): pl.pallas_call(functools.partial(reduce_kernel, units, narr), out_shape=[...  143 us
    pallas_call x1, Pallas kernels, gather_weights(): pl.pallas_call(functools.partial(gather_kernel, specs, order), out_shape=...  90.9 us
    dot_general x16, matrix products, dot(): lax.dot_general(a, b, ((ca, cb), ((), ())), preferred_element_type=F32)  75.2 us
    pallas_call x1, Pallas kernels, attend_back(): pl.pallas_call(functools.partial(attend_back_kernel, span, chunk), grid=(...  61.7 us
    pallas_call x1, Pallas kernels, reduce_rows(): pl.pallas_call(reduce_rows_kernel, out_shape=jax.ShapeDtypeStruct(shape,...  57.1 us
    pallas_call x1, Pallas kernels, gather_rows(): pl.pallas_call(gather_rows_kernel, out_shape=jax.ShapeDtypeStruct((8, *a....  32.2 us
    pallas_call x1, Pallas kernels, attend(): pl.pallas_call(functools.partial(attend_kernel, span, chunk), grid=(rows,...  28.6 us

profile of v1, /device:TPU:0, one launch (start us, length us, event | category | flops | bytes accessed | tf_op | source)
XLA Modules:
  0.0 578.1 jit_solution(15408864631984225015)
XLA Ops:
  6.5 90.9 %gather_weights.1 = (bf16[8,128,896]{2,1,0:T(8,128)(2,1)}, bf16[8,128,1024]{2,1,0:T(8,128)(2,1)}, bf16[8,128,2816]{2,1,0:T(8,128)(2,1)}, bf16[8,128,2816]{2,1,0:T(8,128)(2,1)}, bf16[8,352,1024]{2,1,0:T(8,128)(2,1)}) custom-call(bf16[128,896]{1,0:T(8,128)(2,1)} %pad.4.refs_0_, bf16[128,1024]{1,0:T(8,128)(2,1)} %refs_1_.1, bf16[128,2816]{1,0:T(8,128)(2,1)} %refs_2_.1, ...), custom_call_target="tpu_custom_call" | custom-call | tf_op jit(solution)/shard_map/gather_weights/pallas_call | solution.py:145
  100.9 2.3 fusion.29
  107.5 32.2 %gather_rows.1 = bf16[8,2,320,256]{3,2,1,0:T(8,128)(2,1)} custom-call(bf16[2,320,256]{2,1,0:T(8,128)(2,1)} %pad_maximum_fusion.5.src), custom_call_target="tpu_custom_call" | custom-call | tf_op jit(solution)/shard_map/gather_rows/pallas_call | solution.py:415
  139.7 2.7 fusion.6
  148.3 2.3 slice.173.dl_ref
  153.7 28.6 %attend.1 = (bf16[2,256,1024]{2,1,0:T(8,128)(2,1)}, f32[2,256,128]{2,1,0:T(8,128)}) custom-call(f32[2,8,12,256]{3,2,1,0:T(8,128)} %copy.59.qh_ref, f32[2,384,256]{2,1,0:T(8,128)} %bitcast.157, f32[2,8,8,1024]{3,2,1,0:T(8,128)} %reshape.531.hl_ref, f32[2,8,8,1024]{3,2,1,0:T(8,128)} %reshape.533.hs_ref, bf16[2,256,1024]{2,1,0:T(8,128)(2,1)} %slice.173.dl_ref, ...), custom_call_target="tpu_custom_call" | custom-call | tf_op jit(solution)/shard_map/attend/pallas_call | solution.py:629
  182.3 2.7 multiply_reduce_fusion.2
  185.0 7.7 %fusion.56 = f32[2816,512]{0,1:T(8,128)} fusion(bf16[2816,1024]{1,0:T(8,128)(2,1)} %bitcast.212, bf16[512,1024]{1,0:T(8,128)(2,1)S(1)} %bitcast.169), kind=kOutput, calls=%fused_computation.135 | convolution fusion | flops 2952790016 | bytes 12582912 | tf_op jit(solution)/shard_map/dot_general | solution.py:805
  194.2 8.1 %fusion.55 = f32[512,2816]{1,0:T(8,128)} fusion(bf16[512,1024]{1,0:T(8,128)(2,1)S(1)} %multiply_convert_fusion.1, bf16[1024,2816]{1,0:T(8,128)(2,1)} %bitcast.204), kind=kOutput, calls=%fused_computation.134 | convolution fusion | flops 2952790016 | bytes 12582912 | tf_op jit(solution)/shard_map/dot_general | solution.py:805
  202.3 10.8 %fusion.4 = (bf16[512,2816]{1,0:T(8,128)(2,1)S(1)}, bf16[512,2816]{1,0:T(8,128)(2,1)}, bf16[512,2816]{1,0:T(8,128)(2,1)}) fusion(f32[2816,512]{0,1:T(8,128)} %fusion.56, f32[512,2816]{1,0:T(8,128)} %fusion.55, bf16[512,1024]{1,0:T(8,128)(2,1)S(1)} %multiply_convert_fusion.1, bf16[1024,2816]{1,0:T(8,128)(2,1)S(1)} %bitcast.210), kind=kOutput, calls=%fused_computation.6 | convolution fusion | flops 2975858688 | bytes 27000832 | tf_op jit(solution)/shard_map/dot_general | solution.py:805
  213.2 7.0 %add_convert_fusion = bf16[512,1024]{1,0:T(8,128)(2,1)} fusion(f32[512,1024]{1,0:T(8,128)S(1)} %get-tuple-element.115, bf16[512,2816]{1,0:T(8,128)(2,1)} %get-tuple-element.88, bf16[2816,1024]{1,0:T(8,128)(2,1)S(1)} %bitcast.215), kind=kOutput, calls=%fused_computation.51 | convolution fusion | flops 2953838592 | bytes 11796480 | tf_op jit(solution)/shard_map/dot_general | solution.py:805
  220.2 3.2 fusion.57
  223.4 3.5 multiply_reduce_fusion
  228.8 4.5 convolution_convert_fusion.4
  233.4 61.7 %attend_back.1 = (f32[2,8,12,256]{3,2,1,0:T(8,128)}, f32[2,384,256]{2,1,0:T(8,128)}, f32[2,8,8,1024]{3,2,1,0:T(8,128)}, f32[2,8,8,1024]{3,2,1,0:T(8,128)}, f32[2...) custom-call(f32[2,8,12,256]{3,2,1,0:T(8,128)} %copy.59.qh_ref, f32[2,384,256]{2,1,0:T(8,128)} %bitcast.158, ...), custom_call_target="tpu_custom_call" | custom-call | tf_op jit(solution)/shard_map/attend_back/pallas_call | solution.py:760
  295.1 2.3 reshape.518
  299.2 2.3 concatenate.77
  307.2 2.5 select_convert_fusion
  313.7 2.3 concatenate.74
  317.9 2.9 copy.65
  320.8 2.9 copy.67
  323.7 2.3 fusion.7
  327.4 57.1 %reduce_rows.1 = bf16[2,320,256]{2,1,0:T(8,128)(2,1)S(1)} custom-call(bf16[8,2,320,256]{3,2,1,0:T(8,128)(2,1)S(1)} %fusion.5.src), custom_call_target="tpu_custom_call" | custom-call | tf_op jit(solution)/shard_map/reduce_rows/pallas_call | solution.py:494
  386.9 3.5 fusion.19
  393.5 3.4 bitcast_convert_fusion
  396.9 3.8 copy.73
  400.8 3.4 maximum_maximum_fusion.refs_0_
  404.2 2.7 convolution_convert_fusion.3
  406.9 5.1 convolution_convert_fusion.2
  411.9 5.0 convolution_convert_fusion.1
  417.0 5.0 convolution_convert_fusion
  421.9 142.7 %reduce_weights.1 = (bf16[128,896]{1,0:T(8,128)(2,1)}, bf16[128,1024]{1,0:T(8,128)(2,1)}, bf16[128,2816]{1,0:T(8,128)(2,1)}, bf16[128,2816]{1,0:T(8,128)(2,1)}, bf16[352,1024]{1,0:T(8,128)(2,1)}) custom-call(bf16[8,128,896]{2,1,0:T(8,128)(2,1)} %maximum_maximum_fusion.refs_0_, bf16[8,128,1024]{2,1,0:T(8,128)(2,1)} %bitcast.168, ...), custom_call_target="tpu_custom_call" | custom-call | tf_op jit(solution)/shard_map/reduce_weights/pallas_call | solution.py:365
  (167 shorter events, 59.4 us)
Async XLA Ops:
  6.5 93.1 %copy-start = (bf16[2,256,1024]{2,1,0:T(8,128)(2,1)S(1)}, bf16[2,256,1024]{2,1,0:T(8,128)(2,1)}, u32[]{:S(2)}) copy-start(bf16[2,256,1024]{2,1,0:T(8,128)(2,1)} %param.16) | copy-start | bytes 3145732
  100.9 2.4 copy-start.19
  148.3 4.7 copy-start.22
  153.7 28.6 %copy-start.23 = (bf16[8,128,1024]{2,1,0:T(8,128)(2,1)S(1)}, bf16[8,128,1024]{2,1,0:T(8,128)(2,1)}, u32[]{:S(2)}) copy-start(bf16[8,128,1024]{2,1,0:T(8,128)(2,1)} %get-tuple-element.34) | copy-start | bytes 6291460
  182.3 2.7 copy-start.7
  193.9 8.4 %slice-start.2 = ((s8[5767168]{0:T(1024)(128)(4,1)}), s8[4194304]{0:T(1024)(128)(4,1)S(1)}, s32[]{:S(2)}) async-start(s8[5767168]{0:T(1024)(128)(4,1)} %bitcast.208), calls=%async_computation.2 | async-start | bytes 8388608
  194.1 8.1 %copy-start.5 = (bf16[512,1024]{1,0:T(8,128)(2,1)}, bf16[512,1024]{1,0:T(8,128)(2,1)S(1)}, u32[]{:S(2)}) copy-start(bf16[512,1024]{1,0:T(8,128)(2,1)S(1)} %multiply_convert_fusion.1) | copy-start | bytes 3145732
  194.1 8.1 %slice-start.3 = ((s8[5767168]{0:T(1024)(128)(4,1)}), s8[1572864]{0:T(1024)(128)(4,1)S(1)}, s32[]{:S(2)}) async-start(s8[5767168]{0:T(1024)(128)(4,1)} %bitcast.208), calls=%async_computation.3 | async-start | bytes 3145728
  194.2 19.0 %slice-start.4 = ((s8[5767168]{0:T(1024)(128)(4,1)}), s8[4194304]{0:T(1024)(128)(4,1)S(1)}, s32[]{:S(2)}) async-start(s8[5767168]{0:T(1024)(128)(4,1)} %bitcast.213), calls=%async_computation.4 | async-start | bytes 8388608
  202.3 10.8 %slice-start.5 = ((s8[5767168]{0:T(1024)(128)(4,1)}), s8[1572864]{0:T(1024)(128)(4,1)S(1)}, s32[]{:S(2)}) async-start(s8[5767168]{0:T(1024)(128)(4,1)} %bitcast.213), calls=%async_computation.5 | async-start | bytes 3145728
  202.3 21.1 %slice-start = ((s8[5767168]{0:T(1024)(128)(4,1)}), s8[1572864]{0:T(1024)(128)(4,1)S(1)}, s32[]{:S(2)}) async-start(s8[5767168]{0:T(1024)(128)(4,1)} %bitcast.205), calls=%async_computation | async-start | bytes 3145728
  213.1 10.3 %copy-start.24 = (bf16[512,2816]{1,0:T(8,128)(2,1)}, bf16[512,2816]{1,0:T(8,128)(2,1)S(1)}, u32[]{:S(2)}) copy-start(bf16[512,2816]{1,0:T(8,128)(2,1)S(1)} %get-tuple-element.86) | copy-start | bytes 8650756
  213.1 7.1 %copy-start.27 = (bf16[512,2816]{1,0:T(8,128)(2,1)S(1)}, bf16[512,2816]{1,0:T(8,128)(2,1)}, u32[]{:S(2)}) copy-start(bf16[512,2816]{1,0:T(8,128)(2,1)} %get-tuple-element.87) | copy-start | bytes 8650756
  213.2 10.2 %slice-start.1 = ((s8[5767168]{0:T(1024)(128)(4,1)}), s8[4194304]{0:T(1024)(128)(4,1)S(1)}, s32[]{:S(2)}) async-start(s8[5767168]{0:T(1024)(128)(4,1)} %bitcast.205), calls=%async_computation.1 | async-start | bytes 8388608
  223.4 3.5 copy-start.8
  295.1 8.4 %copy-start.4 = (f32[2,256,1024]{2,1,0:T(8,128)S(1)}, f32[2,256,1024]{2,1,0:T(8,128)}, u32[]{:S(2)}) copy-start(f32[2,256,1024]{2,1,0:T(8,128)} %get-tuple-element.43) | copy-start | bytes 6291460
  323.7 2.3 copy-start.3
  327.4 58.5 %copy-start.12 = (f32[2,384,256]{2,1,0:T(8,128)S(1)}, f32[2,384,256]{2,1,0:T(8,128)}, u32[]{:S(2)}) copy-start(f32[2,384,256]{2,1,0:T(8,128)} %get-tuple-element.40) | copy-start | bytes 2359300
  386.0 4.4 copy-start.16
  386.9 3.6 copy-start.1
  390.5 3.0 copy-start.20
  396.9 3.9 copy-start.11
  400.8 3.4 copy-start.10
  404.2 2.7 copy-start.6
  404.2 2.7 copy-start.28
  406.9 5.1 copy-start.25
  411.9 5.0 copy-start.9
  411.9 5.0 copy-start.26
  564.6 8.8 %copy-start.17 = (bf16[128,1024]{1,0:T(8,128)(2,1)S(1)}, bf16[128,1024]{1,0:T(8,128)(2,1)}, u32[]{:S(2)}) copy-start(bf16[128,1024]{1,0:T(8,128)(2,1)} %get-tuple-element.46) | copy-start | bytes 786436
  564.6 9.6 %copy-start.15 = (bf16[128,2816]{1,0:T(8,128)(2,1)S(1)}, bf16[128,2816]{1,0:T(8,128)(2,1)}, u32[]{:S(2)}) copy-start(bf16[128,2816]{1,0:T(8,128)(2,1)} %get-tuple-element.47) | copy-start | bytes 2162692
  567.1 8.3 %copy-start.14 = (bf16[128,2816]{1,0:T(8,128)(2,1)S(1)}, bf16[128,2816]{1,0:T(8,128)(2,1)}, u32[]{:S(2)}) copy-start(bf16[128,2816]{1,0:T(8,128)(2,1)} %get-tuple-element.48) | copy-start | bytes 2162692
  574.2 2.4 copy-start.13
  (3 other events, 3.7 us)

commit v2 on v1

--- a/solution.py
+++ b/solution.py
@@ -26,15 +26,17 @@
         self.yp = (self.seq, lax.rem(self.batch + 2, 4))
         self.cp = (self.seq, self.batch + 1 - 2 * self.c)
 
+    def along(self, k):
+        return (2 * lax.rem(self.z + k, NZ) + self.x, self.batch)
+
 def greet(me):
     bar = pltpu.get_barrier_semaphore()
     def sig(d):
         pl.semaphore_signal(bar, inc=1, device_id=d, device_id_type=MESH)
-    pl.when(me.z < NZ - 1)(lambda: sig(me.up))
-    pl.when(me.z > 0)(lambda: sig(me.down))
+    for k in range(1, NZ):
+        sig(me.along(k))
     sig(me.xp); sig(me.yp); sig(me.cp)
-    ends = (me.z == 0) | (me.z == NZ - 1)
-    pl.semaphore_wait(bar, jnp.where(ends, 4, 5))
+    pl.semaphore_wait(bar, NZ + 2)
 
 def piece(ref, spec, y, c):
     flow, axis, size = spec
@@ -175,199 +177,185 @@
             idx.append(pl.ds(start[d], size[d]))
     return ref.at[tuple(idx)]
 
-def reduce_kernel(units, narr, *refs):
-    ins, outs = refs[:narr], refs[narr:2 * narr]
-    nu = len(units)
-    pos = 2 * narr
-    A, RC, RY, RX, RZ, RF = [refs[pos + i * nu: pos + (i + 1) * nu] for i in range(6)]
-    pos += 6 * nu
-    ls, cs, cr, ys, yr, xs, xr, zs, zr, fs, fr, os_ = refs[pos:]
-    me = Place()
-    greet(me)
-    def remote(src, dst, ss, rs, dev):
-        return pltpu.make_async_remote_copy(src_ref=src, dst_ref=dst, send_sem=ss, recv_sem=rs, device_id=dev, device_id_type=MESH)
-    def shard_at(i):
-        zz = lax.rem(me.z + 1 + i // 2, NZ)
-        xx = lax.rem(1 - me.x + lax.rem(i, 2), 2)
+class Reduce:
+    def __init__(self, me, units, ins, outs, scratch):
+        self.me, self.units, self.ins, self.outs = me, units, ins, outs
+        nu = len(units)
+        self.A, self.RC, self.RY, self.RX, self.RZ, self.RF = [scratch[i * nu:(i + 1) * nu] for i in range(6)]
+        self.ls, self.cs, self.cr, self.ys, self.yr, self.xs, self.xr, self.zs, self.zr, self.fs, self.fr, self.os_ = scratch[6 * nu:]
+
+    def shard_at(self, i):
+        me = self.me
+        zz = lax.rem(me.z + 1 + lax.rem(i, NZ), NZ)
+        xx = jnp.where(i < NZ, 1 - me.x, me.x)
         return zz, xx, 2 * zz + xx
-    def sub(u, ref, y):
+
+    def sub(self, u, ref, y):
         if u.flow == "R":
             return ref
         n = u.piece[u.axis]
         idx = [slice(None)] * 2
         idx[u.axis] = pl.ds(pl.multiple_of(y * n, n), n)
         return ref.at[tuple(idx)]
-    def core_copy(k, i):
-        u = units[k]; zz, xx, s = shard_at(i)
-        return remote(rect(u, ins[u.arr].at[s], 1 - me.c, 2), RC[k].at[s], cs.at[k, s], cr.at[k, s], me.cp)
-    def local_copy(k, i):
-        u = units[k]; zz, xx, s = shard_at(i)
-        return pltpu.make_async_copy(rect(u, ins[u.arr].at[s], me.c, 2), A[k].at[s], ls.at[k, s])
-    def y_copy(k, i):
-        u = units[k]; zz, xx, s = shard_at(i)
-        return remote(sub(u, A[k].at[s], 1 - me.y), RY[k].at[s], ys.at[k, s], yr.at[k, s], me.yp)
-    def x_copy(k, zz):
-        u = units[k]
-        return remote(sub(u, A[k].at[2 * zz + 1 - me.x], me.y), RX[k].at[zz], xs.at[k, zz], xr.at[k, zz], me.xp)
-    def z_copy(k, d, zz):
-        u = units[k]
-        return remote(sub(u, A[k].at[2 * zz + me.x], me.y), RZ[k].at[d, zz], zs.at[k, d, zz], zr.at[k, d, zz], me.up if d == 0 else me.down)
+
+    def remote(self, src, dst, ss, rs, dev):
+        return pltpu.make_async_remote_copy(src_ref=src, dst_ref=dst, send_sem=ss, recv_sem=rs, device_id=dev, device_id_type=MESH)
+
+    def core_copy(self, k, i):
+        u = self.units[k]; zz, xx, s = self.shard_at(i)
+        return self.remote(rect(u, self.ins[u.arr].at[s], 1 - self.me.c, 2), self.RC[k].at[s], self.cs.at[k, s], self.cr.at[k, s], self.me.cp)
+
+    def local_copy(self, k, i):
+        u = self.units[k]; zz, xx, s = self.shard_at(i)
+        return pltpu.make_async_copy(rect(u, self.ins[u.arr].at[s], self.me.c, 2), self.A[k].at[s], self.ls.at[k, s])
+
+    def y_copy(self, k, i):
+        u = self.units[k]; zz, xx, s = self.shard_at(i)
+        return self.remote(self.sub(u, self.A[k].at[s], 1 - self.me.y), self.RY[k].at[s], self.ys.at[k, s], self.yr.at[k, s], self.me.yp)
+
+    def x_copy(self, k, zz):
+        u, me = self.units[k], self.me
+        return self.remote(self.sub(u, self.A[k].at[2 * zz + 1 - me.x], me.y), self.RX[k].at[zz], self.xs.at[k, zz], self.xr.at[k, zz], me.xp)
+
+    def z_copy(self, k, zz):
+        u, me = self.units[k], self.me
+        return self.remote(self.mine(k, zz), self.RZ[k].at[me.z], self.zs.at[k, zz], self.zr.at[k, me.z], (2 * zz + me.x, me.batch))
+
+    def z_recv(self, k, zz):
+        u, me = self.units[k], self.me
+        return self.remote(self.RZ[k].at[zz], self.RZ[k].at[zz], self.zs.at[k, zz], self.zr.at[k, zz], (2 * zz + me.x, me.batch))
+
+    def mine(self, k, zz):
+        return self.sub(self.units[k], self.A[k].at[2 * zz + self.me.x], self.me.y)
+
+    @staticmethod
     def add(dst, src):
         dst[...] = dst[...] + src[...]
-    def start_core(k):
-        def body(i, c):
-            core_copy(k, i).start()
-            local_copy(k, i).start()
-            return c
-        lax.fori_loop(0, 8, body, 0)
-    def core_stage(k):
-        u = units[k]
-        def body(i, c):
-            zz, xx, s = shard_at(i)
-            local_copy(k, i).wait()
-            core_copy(k, i).wait_recv()
-            add(A[k].at[s], RC[k].at[s])
-            if u.flow == "P":
-                y_copy(k, i).start()
-            else:
-                @pl.when(xx != me.x)
-                def _(): x_copy(k, zz).start()
-            return c
-        lax.fori_loop(0, 8, body, 0)
-    def y_stage(k):
-        u = units[k]
-        def body(i, c):
-            zz, xx, s = shard_at(i)
-            y_copy(k, i).wait_recv()
-            add(sub(u, A[k].at[s], me.y), RY[k].at[s])
-            @pl.when(xx != me.x)
-            def _(): x_copy(k, zz).start()
-            return c
-        lax.fori_loop(0, 8, body, 0)
-    def x_stage(k):
-        u = units[k]
-        def body(i, c):
-            zz = lax.rem(me.z + 1 + i, NZ)
-            x_copy(k, zz).wait_recv()
-            add(sub(u, A[k].at[2 * zz + me.x], me.y), RX[k].at[zz])
-            @pl.when((me.z == 0) & (zz > 0))
-            def _(): z_copy(k, 0, zz).start()
-            @pl.when((me.z == NZ - 1) & (zz < NZ - 1))
-            def _(): z_copy(k, 1, zz).start()
-            return c
-        lax.fori_loop(0, NZ, body, 0)
-    def z_stage(k):
-        u = units[k]
-        def body(i, c):
-            up, down = NZ - 1 - i, i
-            @pl.when((up > me.z) & (me.z > 0))
-            def _():
-                z_copy(k, 0, up).wait_recv()
-                add(sub(u, A[k].at[2 * up + me.x], me.y), RZ[k].at[0, up])
-                z_copy(k, 0, up).start()
-            @pl.when((down < me.z) & (me.z < NZ - 1))
-            def _():
-                z_copy(k, 1, down).wait_recv()
-                add(sub(u, A[k].at[2 * down + me.x], me.y), RZ[k].at[1, down])
-                z_copy(k, 1, down).start()
-            return c
-        lax.fori_loop(0, NZ, body, 0)
-    def fin_y(k):
-        u = units[k]; mine = sub(u, A[k].at[me.seq], me.y)
+
+    def begin(self, k, i):
+        self.core_copy(k, i).start()
+        self.local_copy(k, i).start()
+
+    def core(self, k, i):
+        u = self.units[k]; zz, xx, s = self.shard_at(i)
+        self.local_copy(k, i).wait()
+        self.core_copy(k, i).wait_recv()
+        self.add(self.A[k].at[s], self.RC[k].at[s])
         if u.flow == "P":
-            dst = rect(u, outs[u.arr], 2 * me.c + me.y, 4)
-            return remote(mine, dst, fs.at[k, 0], fr.at[k, 0], me.yp)
-        return remote(mine, RF[k], fs.at[k, 0], fr.at[k, 0], me.yp)
-    def fin_c(k, w):
-        u = units[k]
+            self.y_copy(k, i).start()
+        else:
+            pl.when(i < NZ)(lambda: self.x_copy(k, zz).start())
+
+    def y(self, k, i):
+        u = self.units[k]; zz, xx, s = self.shard_at(i)
+        self.y_copy(k, i).wait_recv()
+        self.add(self.sub(u, self.A[k].at[s], self.me.y), self.RY[k].at[s])
+        pl.when(i < NZ)(lambda: self.x_copy(k, zz).start())
+
+    def x(self, k, i):
+        me = self.me
+        zz = lax.rem(me.z + 1 + i, NZ)
+        self.x_copy(k, zz).wait_recv()
+        self.add(self.mine(k, zz), self.RX[k].at[zz])
+        pl.when(zz != me.z)(lambda: self.z_copy(k, zz).start())
+
+    def fin_y(self, k):
+        u, me = self.units[k], self.me
+        mine = self.mine(k, me.z)
+        dst = rect(u, self.outs[u.arr], 2 * me.c + me.y, 4) if u.flow == "P" else self.RF[k]
+        return self.remote(mine, dst, self.fs.at[k, 0], self.fr.at[k, 0], me.yp)
+
+    def fin_c(self, k, w):
+        u, me = self.units[k], self.me
         if u.flow == "P":
             if w == 0:
-                return remote(sub(u, A[k].at[me.seq], me.y), rect(u, outs[u.arr], 2 * me.c + me.y, 4), fs.at[k, 1], fr.at[k, 1], me.cp)
-            v = rect(u, outs[u.arr], 2 * me.c + 1 - me.y, 4)
-            return remote(v, v, fs.at[k, 2], fr.at[k, 2], me.cp)
-        v = rect(u, outs[u.arr], me.c, 2)
-        return remote(RF[k], v, fs.at[k, 1], fr.at[k, 1], me.cp)
-    def out_copy(k):
-        u = units[k]
+                return self.remote(self.mine(k, me.z), rect(u, self.outs[u.arr], 2 * me.c + me.y, 4), self.fs.at[k, 1], self.fr.at[k, 1], me.cp)
+            v = rect(u, self.outs[u.arr], 2 * me.c + 1 - me.y, 4)
+            return self.remote(v, v, self.fs.at[k, 2], self.fr.at[k, 2], me.cp)
+        return self.remote(self.RF[k], rect(u, self.outs[u.arr], me.c, 2), self.fs.at[k, 1], self.fr.at[k, 1], me.cp)
+
+    def out_copy(self, k):
+        u, me = self.units[k], self.me
         if u.flow == "P":
-            return pltpu.make_async_copy(sub(u, A[k].at[me.seq], me.y), rect(u, outs[u.arr], 2 * me.c + me.y, 4), os_.at[k])
-        return pltpu.make_async_copy(RF[k], rect(u, outs[u.arr], me.c, 2), os_.at[k])
-    def own_stage(k):
-        u = units[k]
-        @pl.when(me.z > 0)
-        def _():
-            z_copy(k, 0, me.z).wait_recv()
-            add(sub(u, A[k].at[me.seq], me.y), RZ[k].at[0, me.z])
-        @pl.when(me.z < NZ - 1)
-        def _():
-            z_copy(k, 1, me.z).wait_recv()
-            add(sub(u, A[k].at[me.seq], me.y), RZ[k].at[1, me.z])
-        fin_y(k).start()
-        if u.flow == "P":
-            out_copy(k).start()
-            fin_c(k, 0).start()
-    def last_stage(k):
-        u = units[k]
-        fin_y(k).wait_recv()
-        if u.flow == "P":
-            fin_c(k, 1).start()
+            return pltpu.make_async_copy(self.mine(k, me.z), rect(u, self.outs[u.arr], 2 * me.c + me.y, 4), self.os_.at[k])
+        return pltpu.make_async_copy(self.RF[k], rect(u, self.outs[u.arr], me.c, 2), self.os_.at[k])
+
+    def own(self, k, i):
+        me = self.me
+        def body(i, c):
+            zz = lax.rem(me.z + i, NZ)
+            self.z_recv(k, zz).wait_recv()
+            self.add(self.mine(k, me.z), self.RZ[k].at[zz])
+            return c
+        lax.fori_loop(1, NZ, body, 0)
+        self.fin_y(k).start()
+        if self.units[k].flow == "P":
+            self.out_copy(k).start()
+            self.fin_c(k, 0).start()
+
+    def last(self, k, i):
+        self.fin_y(k).wait_recv()
+        if self.units[k].flow == "P":
+            self.fin_c(k, 1).start()
         else:
-            add(RF[k], A[k].at[me.seq])
-            out_copy(k).start()
-            fin_c(k, 0).start()
-    def end_stage(k):
-        u = units[k]
-        fin_c(k, 0).wait_recv()
-        fin_c(k, 0).wait_send()
-        if u.flow == "P":
-            fin_c(k, 1).wait_recv()
-            fin_c(k, 1).wait_send()
-        out_copy(k).wait()
-        fin_y(k).wait_send()
+            self.add(self.RF[k], self.mine(k, self.me.z))
+            self.out_copy(k).start()
+            self.fin_c(k, 0).start()
+
+    def end(self, k, i):
+        me = self.me
+        flow = self.units[k].flow
+        for w in range(2 if flow == "P" else 1):
+            self.fin_c(k, w).wait_recv()
+            self.fin_c(k, w).wait_send()
+        self.out_copy(k).wait()
+        self.fin_y(k).wait_send()
         def body(i, c):
-            core_copy(k, i).wait_send()
-            if u.flow == "P": y_copy(k, i).wait_send()
+            self.core_copy(k, i).wait_send()
+            if flow == "P": self.y_copy(k, i).wait_send()
             return c
         lax.fori_loop(0, 8, body, 0)
         def body(zz, c):
-            x_copy(k, zz).wait_send()
-            @pl.when((zz > me.z))
-            def _(): z_copy(k, 0, zz).wait_send()
-            @pl.when((zz < me.z))
-            def _(): z_copy(k, 1, zz).wait_send()
+            self.x_copy(k, zz).wait_send()
+            pl.when(zz != me.z)(lambda: self.z_copy(k, zz).wait_send())
             return c
         lax.fori_loop(0, NZ, body, 0)
-    for k in range(nu): start_core(k)
-    for k in range(nu): core_stage(k)
-    Ps = [k for k in range(nu) if units[k].flow == "P"]
-    Rs = [k for k in range(nu) if units[k].flow == "R"]
-    for i in range(max(len(Ps), len(Rs))):
-        if i < len(Ps): y_stage(Ps[i])
-        if i < len(Rs): x_stage(Rs[i]);
-        if i < len(Rs): z_stage(Rs[i])
-    for k in Rs: own_stage(k)
-    for k in Ps:
-        x_stage(k); z_stage(k)
-    for k in Rs: last_stage(k)
-    for k in Ps: own_stage(k)
-    for k in Ps: last_stage(k)
-    for k in range(nu): end_stage(k)
-
-def reduce_weights(arrays, units, cid):
-    narr, nu = len(arrays), len(units)
+
+    def run(self, plan):
+        for step, k, first, n in plan:
+            fn = getattr(self, step)
+            if n == 1:
+                fn(k, first)
+            else:
+                def body(i, c):
+                    fn(k, i)
+                    return c
+                lax.fori_loop(first, first + n, body, 0)
+
+def reduce_kernel(units, narr, plan, *refs):
+    me = Place()
+    greet(me)
+    red = Reduce(me, units, refs[:narr], refs[narr:2 * narr], refs[2 * narr:])
+    red.run(plan)
+
+def reduce_scratch(units):
+    nu = len(units)
     DMA = pltpu.SemaphoreType.DMA
     bf = jnp.bfloat16
     V = pltpu.VMEM
-    scratch = ([V((8, *u.half), bf) for u in units] + [V((8, *u.half), bf) for u in units]
+    return ([V((8, *u.half), bf) for u in units] + [V((8, *u.half), bf) for u in units]
         + [V((8, *u.piece) if u.flow == "P" else (16, 128), bf) for u in units] + [V((4, *u.piece), bf) for u in units]
-        + [V((2, 4, *u.piece), bf) for u in units] + [V(u.piece if u.flow == "R" else (16, 128), bf) for u in units]
-        + [DMA((nu, 8))] * 5 + [DMA((nu, 4))] * 2 + [DMA((nu, 2, 4))] * 2 + [DMA((nu, 3))] * 2 + [DMA((nu,))])
+        + [V((4, *u.piece), bf) for u in units] + [V(u.piece if u.flow == "R" else (16, 128), bf) for u in units]
+        + [DMA((nu, 8))] * 5 + [DMA((nu, 4))] * 4 + [DMA((nu, 3))] * 2 + [DMA((nu,))])
+
+def reduce_weights(arrays, units, plan, cid):
+    narr = len(arrays)
     return pl.pallas_call(
-        functools.partial(reduce_kernel, units, narr),
+        functools.partial(reduce_kernel, units, narr, plan),
         out_shape=[jax.ShapeDtypeStruct(a.shape[1:], a.dtype) for a in arrays],
         in_specs=[pl.BlockSpec(memory_space=pl.ANY)] * narr,
         out_specs=[pl.BlockSpec(memory_space=pl.ANY)] * narr,
-        scratch_shapes=scratch,
+        scratch_shapes=reduce_scratch(units),
         compiler_params=pltpu.CompilerParams(collective_id=cid, has_side_effects=True, vmem_limit_bytes=58 << 20),
         name="reduce_weights",
     )(*arrays)
@@ -641,6 +629,29 @@
 def attend_back_kernel(span, chunk, qh_ref, qr_ref, hl_ref, hs_ref, dl_ref, ds_ref, cond_ref, bl_ref, bs_ref, lse_ref, o_ref, g_ref,
                        dqh_ref, dqr_ref, dhl_ref, dhs_ref, ddl_ref, dds_ref):
     p = pl.program_id(1)
+    @pl.when(p == 0)
+    def _():
+        dqr_ref[...] = jnp.zeros_like(dqr_ref)
+        ddl_ref[...] = jnp.zeros_like(ddl_ref)
+        dds_ref[...] = jnp.zeros_like(dds_ref)
+    pair_back(span, chunk, p, qh_ref, qr_ref, Pair(hl_ref, 0, 0), Pair(hs_ref, 0, 0), dl_ref, ds_ref, cond_ref, bl_ref, bs_ref, lse_ref, o_ref, g_ref,
+              dqh_ref, dqr_ref, Pair(dhl_ref, 0, 0), Pair(dhs_ref, 0, 0), ddl_ref, dds_ref)
+
+class Pair:
+    def __init__(self, ref, *at):
+        self.ref, self.at = ref, at
+
+    def all(self):
+        return self.ref[self.at]
+
+    def row(self, j, sl):
+        return self.ref[(*self.at, slice(j, j + 1), sl)]
+
+    def put(self, j, sl, value):
+        self.ref[(*self.at, slice(j, j + 1), sl)] = value
+
+def pair_back(span, chunk, p, qh_ref, qr_ref, hl, hs, dl_ref, ds_ref, cond_ref, bl_ref, bs_ref, lse_ref, o_ref, g_ref,
+              dqh_ref, dqr_ref, dhl, dhs, ddl_ref, dds_ref):
     n2 = 2 * span
     nk = dl_ref.shape[-1]
     qh, qr = qh_ref[0, 0], qr_ref[0]
@@ -669,28 +680,22 @@
     l1 = jnp.sum(jnp.where(lane == 2 * p + 1, lse, 0.0), -1, keepdims=True)
     dello, delhi = jnp.concatenate([d0[:span], d1[:span]], 0), jnp.concatenate([d0[span:], d1[span:]], 0)
     lselo, lsehi = jnp.concatenate([l0[:span], l1[:span]], 0), jnp.concatenate([l0[span:], l1[span:]], 0)
-    heads = (hl_ref[0, 0], hs_ref[0, 0])
+    heads = (hl.all(), hs.all())
     dims = (dl_ref[0], ds_ref[0])
     cond = cond_ref[...]
     klo, ksel = pair_factors(heads, dims, cond, 0, 0)
     vlo, vsel = pair_factors(heads, dims, cond, 4, 128)
     tri = causal_bias(n2, span)
 
-    @pl.when(p == 0)
-    def _():
-        dqr_ref[...] = jnp.zeros_like(dqr_ref)
-        ddl_ref[...] = jnp.zeros_like(ddl_ref)
-        dds_ref[...] = jnp.zeros_like(dds_ref)
-
-    def put(dkt, h_ref, d_ref, hd_ref, dd_ref, base, at, sl):
+    def put(dkt, h, d_ref, hd, dd_ref, base, at, sl):
         for r in range(2):
             dim = d_ref[0, at + 64 * r:at + 64 * r + 64, sl].astype(F32)
             total = None
-            for h in range(2):
-                part = dkt[64 * h:64 * h + 64]
-                j = base + 2 * r + h
-                hd_ref[0, 0, j:j + 1, sl] = jnp.sum(part * dim, 0, keepdims=True) * 0.5
-                term = part * h_ref[0, 0, j:j + 1, sl]
+            for k in range(2):
+                part = dkt[64 * k:64 * k + 64]
+                j = base + 2 * r + k
+                hd.put(j, sl, jnp.sum(part * dim, 0, keepdims=True) * 0.5)
+                term = part * h.row(j, sl)
                 total = term if total is None else total + term
             dd_ref[0, at + 64 * r:at + 64 * r + 64, sl] += total * 0.5
 
@@ -716,8 +721,8 @@
         if c == 0:
             dk = jnp.concatenate([dk[:, :span] + dk3, dk[:, span:]], 1)
             dv = jnp.concatenate([dv[:, :span] + dv3, dv[:, span:]], 1)
-        put(dk, hl_ref, dl_ref, dhl_ref, ddl_ref, 0, 0, sl)
-        put(dv, hl_ref, dl_ref, dhl_ref, ddl_ref, 4, 128, sl)
+        put(dk, hl, dl_ref, dhl, ddl_ref, 0, 0, sl)
+        put(dv, hl, dl_ref, dhl, ddl_ref, 4, 128, sl)
     for c in range(0, nk, chunk):
         sl = slice(c, c + chunk)
         on = cond[:, sl] > 0.5
@@ -733,8 +738,8 @@
         dv = nn(gtboth, pb)
         dk = jnp.where(on, dk[:128], dk[128:])
         dv = jnp.where(on, dv[:128], dv[128:])
-        put(dk, hs_ref, ds_ref, dhs_ref, dds_ref, 0, 0, sl)
-        put(dv, hs_ref, ds_ref, dhs_ref, dds_ref, 4, 128, sl)
+        put(dk, hs, ds_ref, dhs, dds_ref, 0, 0, sl)
+        put(dv, hs, ds_ref, dhs, dds_ref, 4, 128, sl)
     dqlo = unstack_heads(dq2[:, :128] + dq3)
     dqhi = unstack_heads(dq2[:, 128:] + dq1)
     dqt = (jnp.concatenate([dqlo, dqhi], 0) * (0.125 / 6.0)).T
@@ -769,6 +774,159 @@
         name="attend_back",
     )(qh, qr, hl, hs, dl, ds, cond, bl, bs, lse, o, g)
 
+class Rows:
+    def __init__(self, me, pack, out, RX, RZ, xs, xr, zs, zr):
+        self.me, self.pack, self.out, self.RX, self.RZ = me, pack, out, RX, RZ
+        self.xs, self.xr, self.zs, self.zr = xs, xr, zs, zr
+
+    def remote(self, src, dst, ss, rs, dev):
+        return pltpu.make_async_remote_copy(src_ref=src, dst_ref=dst, send_sem=ss, recv_sem=rs, device_id=dev, device_id_type=MESH)
+
+    def x_copy(self, b, zz):
+        return self.remote(self.pack.at[b, 2 * zz + 1 - self.me.x], self.RX.at[b, zz], self.xs.at[b, zz], self.xr.at[b, zz], self.me.xp)
+
+    def z_copy(self, b, zz):
+        me = self.me
+        return self.remote(self.mine(b, zz), self.RZ.at[b, me.z], self.zs.at[b, zz], self.zr.at[b, me.z], (2 * zz + me.x, me.batch))
+
+    def z_recv(self, b, zz):
+        me = self.me
+        return self.remote(self.RZ.at[b, zz], self.RZ.at[b, zz], self.zs.at[b, zz], self.zr.at[b, zz], (2 * zz + me.x, me.batch))
+
+    def mine(self, b, zz):
+        return self.pack.at[b, 2 * zz + self.me.x]
+
+    @staticmethod
+    def add(dst, src):
+        dst[...] = dst[...] + src[...]
+
+    def begin(self, b):
+        def body(i, c):
+            self.x_copy(b, lax.rem(self.me.z + 1 + i, NZ)).start()
+            return c
+        lax.fori_loop(0, NZ, body, 0)
+
+    def x(self, b):
+        me = self.me
+        def body(i, c):
+            zz = lax.rem(me.z + 1 + i, NZ)
+            self.x_copy(b, zz).wait_recv()
+            self.add(self.mine(b, zz), self.RX.at[b, zz])
+            pl.when(zz != me.z)(lambda: self.z_copy(b, zz).start())
+            return c
+        lax.fori_loop(0, NZ, body, 0)
+
+    def own(self, b):
+        me = self.me
+        def body(i, c):
+            zz = lax.rem(me.z + i, NZ)
+            self.z_recv(b, zz).wait_recv()
+            self.add(self.mine(b, me.z), self.RZ.at[b, zz])
+            return c
+        lax.fori_loop(1, NZ, body, 0)
+        self.out[b] = self.pack[b, me.seq]
+
+    def end(self, b):
+        me = self.me
+        def sent(zz, c):
+            self.x_copy(b, zz).wait_send()
+            pl.when(zz != me.z)(lambda: self.z_copy(b, zz).wait_send())
+            return c
+        lax.fori_loop(0, NZ, sent, 0)
+
+def lay_out(me, shared_ref, b, span, cond_ref, dl, ds, hl, hs):
+    n = shared_ref.shape[0]
+    for i in range(n):
+        j = lax.rem(me.seq + i, n)
+        sl = slice(i * span, (i + 1) * span)
+        on = cond_ref[:, sl] > 0.5
+        low = shared_ref[j, b, :256, :span].astype(F32)
+        high = shared_ref[j, b, :256, span:].astype(F32)
+        dl[0, :, sl] = low.astype(BF16)
+        ds[0, :, sl] = jnp.where(on, low, high).astype(BF16)
+        low = shared_ref[j, b, 256:, :span].astype(F32)
+        high = shared_ref[j, b, 256:, span:].astype(F32)
+        hl[:, :, sl] = low.reshape(PAIRS, 8, span)
+        hs[:, :, sl] = jnp.where(on, low, high).reshape(PAIRS, 8, span)
+
+def pack_up(me, b, span, cond_ref, pack, ddl, dds, dhl, dhs):
+    n = pack.shape[1]
+    for i in range(n):
+        j = lax.rem(me.seq + i, n)
+        sl = slice(i * span, (i + 1) * span)
+        on = cond_ref[:, sl] > 0.5
+        for at, lo, se in ((0, ddl[0, :, sl], dds[0, :, sl]), (256, dhl[:, :, sl].reshape(64, span), dhs[:, :, sl].reshape(64, span))):
+            rows = slice(at, at + lo.shape[0])
+            pack[b, j, rows, :span] = (lo + jnp.where(on, se, 0.0)).astype(BF16)
+            pack[b, j, rows, span:] = jnp.where(on, 0.0, se).astype(BF16)
+
+def back_kernel(span, chunk, units, narr, plan, qh_ref, qr_ref, shared_ref, cond_ref, bl_ref, bs_ref, lse_ref, o_ref, g_ref, *refs):
+    ins = refs[:narr]
+    dqh_ref, dqr_ref, mine_ref = refs[narr:narr + 3]
+    outs = refs[narr + 3:2 * narr + 3]
+    dl, ds, hl, hs, ddl, dds, dhl, dhs, pack, RX, RZ, xs, xr, zs, zr = refs[2 * narr + 3:2 * narr + 18]
+    me = Place()
+    b, p = pl.program_id(0), pl.program_id(1)
+    step = b * PAIRS + p
+    red = Reduce(me, units, ins, outs, refs[2 * narr + 18:])
+    row = Rows(me, pack, mine_ref, RX, RZ, xs, xr, zs, zr)
+
+    @pl.when(step == 0)
+    def _():
+        greet(me)
+        red.run(plan["first"])
+
+    @pl.when(p == 0)
+    def _():
+        lay_out(me, shared_ref, b, span, cond_ref, dl, ds, hl, hs)
+        dqr_ref[...] = jnp.zeros_like(dqr_ref)
+        ddl[...] = jnp.zeros_like(ddl)
+        dds[...] = jnp.zeros_like(dds)
+
+    pair_back(span, chunk, p, qh_ref, qr_ref, Pair(hl, p), Pair(hs, p), dl, ds, cond_ref, bl_ref, bs_ref, lse_ref, o_ref, g_ref, dqh_ref, dqr_ref, Pair(dhl, p), Pair(dhs, p), ddl, dds)
+
+    @pl.when(p == PAIRS - 1)
+    def _():
+        pack_up(me, b, span, cond_ref, pack, ddl, dds, dhl, dhs)
+        row.begin(b)
+
+    def act(items):
+        for it in items:
+            if it[0] == "row":
+                getattr(row, it[1])(it[2])
+            else:
+                red.run([it])
+    for s, items in plan["steps"].items():
+        pl.when(step == s)(functools.partial(act, items))
+
+def attend_back_reduce(qh, qr, shared, cond, bl, bs, lse, o, g, grads, units, plan, cid):
+    rows, pairs, _, nq = qh.shape
+    n = shared.shape[0]
+    span = nq // 2
+    nk = n * span
+    narr, nu = len(grads), len(units)
+    full = lambda *s: pl.BlockSpec((1, *s), lambda b, p: (b, *([0] * len(s))))
+    pairb = lambda *s: pl.BlockSpec((1, 1, *s), lambda b, p: (b, p, *([0] * len(s))))
+    tok = pl.BlockSpec((1, nq, 128), lambda b, p: (b, 0, p))
+    sd = jax.ShapeDtypeStruct
+    DMA = pltpu.SemaphoreType.DMA
+    V = pltpu.VMEM
+    whole = pl.BlockSpec(memory_space=pltpu.VMEM)
+    far = pl.BlockSpec(memory_space=pl.ANY)
+    part = shared.shape[2:]
+    scratch = [V((1, 256, nk), BF16)] * 2 + [V((PAIRS, 8, nk), F32)] * 2 + [V((1, 256, nk), F32)] * 2 + [V((PAIRS, 8, nk), F32)] * 2
+    scratch += [V((rows, n, *part), BF16), V((rows, NZ, *part), BF16), V((rows, NZ, *part), BF16)] + [DMA((rows, NZ))] * 4
+    return pl.pallas_call(
+        functools.partial(back_kernel, span, min(512, nk), units, narr, plan),
+        grid=(rows, pairs),
+        out_shape=[sd((rows, pairs, 12, nq), F32), sd((rows, 384, nq), F32), sd((rows, *part), BF16)] + [sd(a.shape[1:], BF16) for a in grads],
+        in_specs=[pairb(12, nq), full(384, nq), whole, pl.BlockSpec((1, nk), lambda b, p: (0, 0)), full(1, nk), full(1, nk), full(nq, 128), tok, tok] + [far] * narr,
+        out_specs=[pairb(12, nq), full(384, nq), whole] + [far] * narr,
+        scratch_shapes=scratch + reduce_scratch(units),
+        compiler_params=pltpu.CompilerParams(collective_id=cid, has_side_effects=True, vmem_limit_bytes=60 << 20),
+        name="attend_back_reduce",
+    )(qh, qr, shared, cond, bl, bs, lse, o, g, *grads)
+
 HEADS, HDIM, QRANK, KVRANK = 16, 64, 6, 2
 PAIRS = HEADS // 2
 EPSILON = 1e-06
@@ -805,22 +963,40 @@
     return lax.dot_general(a, b, ((ca, cb), ((), ())), preferred_element_type=F32)
 
 
-def pair_rows(a, ranks):
-    rows, _, n = a.shape
-    return a.reshape(rows, ranks, PAIRS, 2, n).transpose(0, 2, 1, 3, 4).reshape(rows, PAIRS, ranks * 2, n)
-
-
-def unpair_rows(a, ranks):
-    rows, _, _, n = a.shape
-    return a.reshape(rows, PAIRS, ranks, 2, n).transpose(0, 2, 1, 3, 4).reshape(rows, ranks * HEADS, n)
+def pair_columns(a, ranks):
+    return a.reshape(-1, ranks, PAIRS, 2).transpose(0, 2, 1, 3).reshape(a.shape)
+
+
+def head_columns(a, ranks):
+    return a.reshape(-1, PAIRS, ranks, 2).transpose(0, 2, 1, 3).reshape(a.shape)
 
 
 GATHER_SPECS = [("R", 0, 128), ("P", 0, 128), ("P", 0, 128), ("R", 0, 128), ("P", 1, 1024)]
 REDUCE_UNITS = [
-    Unit(4, (0, 176), (0, 1024), "P", 1), Unit(3, (0, 128), (0, 1408), "R", 0),
-    Unit(4, (176, 176), (0, 1024), "P", 1), Unit(3, (0, 128), (1408, 1408), "R", 0),
-    Unit(2, (0, 128), (0, 1408), "P", 0), Unit(1, (0, 128), (0, 1024), "R", 0),
-    Unit(2, (0, 128), (1408, 1408), "P", 0), Unit(0, (0, 128), (0, 896), "R", 0)]
+    Unit(3, (0, 176), (0, 1024), "P", 1), Unit(2, (0, 128), (0, 1408), "R", 0),
+    Unit(3, (176, 176), (0, 1024), "P", 1), Unit(2, (0, 128), (1408, 1408), "R", 0),
+    Unit(1, (0, 128), (0, 1408), "P", 0), Unit(1, (0, 128), (1408, 1408), "P", 0),
+    Unit(0, (0, 128), (0, 1024), "P", 0)]
+REDUCE_PLAN = {
+    "first": [("begin", 0, 0, 8), ("begin", 1, 0, 8), ("begin", 2, 0, 8), ("begin", 3, 0, 8), ("begin", 4, 0, 8), ("begin", 5, 0, 8), ("begin", 6, 0, 8), ("core", 0, 0, 4), ("core", 0, 4, 4), ("core", 1, 0, 4)],
+    "steps": {
+        0: [("core", 1, 4, 4)],
+        1: [("core", 3, 0, 4), ("core", 2, 0, 4), ("x", 1, 0, 4)],
+        2: [("core", 4, 4, 4)],
+        3: [("core", 2, 4, 4), ("y", 2, 0, 4)],
+        4: [("core", 3, 4, 4), ("x", 3, 0, 4)],
+        5: [("core", 5, 4, 4), ("y", 2, 4, 4), ("core", 4, 0, 4), ("core", 5, 0, 4), ("y", 0, 0, 4), ("core", 6, 4, 4)],
+        6: [("x", 2, 0, 4)],
+        7: [("y", 0, 4, 4)],
+        8: [("x", 0, 0, 4)],
+        9: [("y", 4, 0, 4), ("row", "x", 0), ("y", 5, 0, 4), ("core", 6, 0, 4)],
+        10: [("y", 6, 4, 4), ("y", 4, 4, 4), ("y", 5, 4, 4)],
+        11: [("x", 4, 0, 4)],
+        13: [("y", 6, 0, 4), ("own", 0, 0, 1), ("x", 5, 0, 4), ("own", 3, 0, 1)],
+        15: [("own", 1, 0, 1), ("own", 4, 0, 1), ("own", 2, 0, 1), ("x", 6, 0, 4), ("own", 5, 0, 1), ("last", 3, 0, 1), ("row", "x", 1), ("own", 6, 0, 1), ("row", "own", 0), ("last", 1, 0, 1), ("last", 6, 0, 1), ("last", 2, 0, 1), ("last", 5, 0, 1), ("last", 4, 0, 1), ("last", 0, 0, 1), ("row", "own", 1), ("end", 0, 0, 1), ("end", 1, 0, 1), ("end", 2, 0, 1), ("end", 3, 0, 1), ("end", 4, 0, 1), ("end", 5, 0, 1), ("end", 6, 0, 1), ("row", "end", 0), ("row", "end", 1)],
+    }}
+SMALL_UNITS = [Unit(0, (0, 128), (0, 896), "P", 0)]
+SMALL_PLAN = [("begin", 0, 0, 8), ("core", 0, 0, 8), ("y", 0, 0, 8), ("x", 0, 0, 4), ("own", 0, 0, 1), ("last", 0, 0, 1), ("end", 0, 0, 1)]
 
 
 def gather_all(near, arrays):
@@ -829,9 +1005,7 @@
     return [lax.all_gather(a, "seq", axis=0) for a in arrays]
 
 
-def reduce_all(near, arrays):
-    if near:
-        return reduce_weights(arrays, REDUCE_UNITS, 1)
+def reduce_far(arrays):
     out = []
     for a in arrays:
         own = lax.psum_scatter(a.astype(F32), "seq", scatter_dimension=0, tiled=True)[0]
@@ -847,7 +1021,8 @@
     nseq = span_order.shape[0]
     nk = nseq * span
     me = lax.axis_index("seq")
-    small = jnp.concatenate([query_heads, query_dims, key_dims, value_dims, key_heads, value_heads, attn_gain[:, None], ffn_gain[:, None]], 1)
+    key_value_heads = pair_columns(jnp.concatenate([key_heads, value_heads], 1), 4)
+    small = jnp.concatenate([pair_columns(query_heads, QRANK), query_dims, key_dims, value_dims, key_value_heads, attn_gain[:, None], ffn_gain[:, None]], 1)
     small = jnp.pad(small, ((0, 0), (0, 896 - small.shape[1])))
     parts = gather_all(near, [small, out_proj, gate_proj, up_proj, down_proj])
     small, w_out, w_gate, w_up, w_down = [p.reshape(-1, p.shape[-1]) for p in parts]
@@ -876,14 +1051,16 @@
     qr = rotate(factors[:, 96:480], cosine, sine)
     own = jnp.concatenate([rotate(factors[:, 480:608], cosine, sine), factors[:, 608:800]], 1).astype(BF16)
     shared = gather_rows(own, 2) if near else lax.all_gather(own, "seq", axis=0)
-    shared = lax.dynamic_slice_in_dim(jnp.concatenate([shared, shared], 0), me, nseq, 0)
-    low, high = shared[..., :span], shared[..., span:]
+    turned = lax.dynamic_slice_in_dim(jnp.concatenate([shared, shared], 0), me, nseq, 0)
+    low, high = turned[..., :span], turned[..., span:]
     sel = jnp.where(chosen[:, None, None, None], low, high)
     low = low.transpose(1, 2, 0, 3).reshape(rows, 320, nk)
     sel = sel.transpose(1, 2, 0, 3).reshape(rows, 320, nk)
-    att = (pair_rows(qh, QRANK), qr, pair_rows(low[:, 256:].astype(F32), 4), pair_rows(sel[:, 256:].astype(F32), 4),
-           low[:, :256], sel[:, :256], cond, low_bias, sel_bias)
-    heads_out, lse = attend(*att)
+    qh = qh.reshape(rows, PAIRS, 12, slots)
+    in_pairs = lambda a: a[:, 256:].astype(F32).reshape(rows, PAIRS, 8, nk)
+    factors = (in_pairs(low), in_pairs(sel), low[:, :256], sel[:, :256])
+    masks = (cond, low_bias, sel_bias)
+    heads_out, lse = attend(qh, qr, *factors, *masks)
     heads_flat = heads_out.reshape(count, width)
 
     resid = flat + dot(heads_flat, w_out, (1,), (0,))
@@ -909,26 +1086,33 @@
     out_grad = dot(heads_flat, d_attn, (0,), (0,)).astype(BF16)
     d_heads = dot(d_attn, w_out, (1,), (1,)).astype(BF16).reshape(rows, slots, width)
 
-    dqh, dqr, dhl, dhs, ddl, dds = attend_back(*att, lse, heads_out, d_heads)
-    from_low = jnp.concatenate([ddl, unpair_rows(dhl, 4)], 1).reshape(rows, 320, nseq, span)
-    from_sel = jnp.concatenate([dds, unpair_rows(dhs, 4)], 1).reshape(rows, 320, nseq, span)
-    pick = chosen[None, None, :, None]
-    both = jnp.concatenate([from_low + jnp.where(pick, from_sel, 0.0), jnp.where(pick, 0.0, from_sel)], -1)
-    both = both.astype(BF16) if near else both
-    both = both.transpose(2, 0, 1, 3)
-    both = lax.dynamic_slice_in_dim(jnp.concatenate([both, both], 0), lax.rem(nseq - me, nseq), nseq, 0)
-    mine = (reduce_rows(both, 3) if near else lax.psum_scatter(both, "seq", scatter_dimension=0, tiled=True)[0]).astype(F32)
-    turned = jnp.concatenate([unpair_rows(dqh, QRANK), rotate(dqr, cosine, -sine), rotate(mine[:, :128], cosine, -sine), mine[:, 128:]], 1).astype(BF16)
+    grads = [g.reshape(nseq, -1, g.shape[-1]) for g in (out_grad, gate_grad, up_grad, down_grad)]
+    if near:
+        dqh, dqr, mine, *sums = attend_back_reduce(qh, qr, shared, *masks, lse, heads_out, d_heads, grads, REDUCE_UNITS, REDUCE_PLAN, 1)
+    else:
+        dqh, dqr, dhl, dhs, ddl, dds = attend_back(qh, qr, *factors, *masks, lse, heads_out, d_heads)
+        from_low = jnp.concatenate([ddl, dhl.reshape(rows, 64, nk)], 1).reshape(rows, 320, nseq, span)
+        from_sel = jnp.concatenate([dds, dhs.reshape(rows, 64, nk)], 1).reshape(rows, 320, nseq, span)
+        pick = chosen[None, None, :, None]
+        both = jnp.concatenate([from_low + jnp.where(pick, from_sel, 0.0), jnp.where(pick, 0.0, from_sel)], -1).transpose(2, 0, 1, 3)
+        both = lax.dynamic_slice_in_dim(jnp.concatenate([both, both], 0), lax.rem(nseq - me, nseq), nseq, 0)
+        mine = lax.psum_scatter(both, "seq", scatter_dimension=0, tiled=True)[0]
+        sums = reduce_far(grads)
+    mine = mine.astype(F32)
+    turned = jnp.concatenate([dqh.reshape(rows, 96, slots), rotate(dqr, cosine, -sine), rotate(mine[:, :128], cosine, -sine), mine[:, 128:]], 1).astype(BF16)
     small_grad = dot(by_row, turned, (0, 1), (0, 2))
     d_normed = dot(turned, w_qkv, (1,), (1,)).reshape(count, width)
     d_first, gain_one_grad = rms_backward(d_normed, unit_one, scale_one, gain_one)
     input_grad = (d_resid + d_first).reshape(rows, slots, width)
     small_grad = jnp.concatenate([small_grad, gain_one_grad[:, None], gain_two_grad[:, None], jnp.zeros((width, 94), F32)], 1).astype(BF16)
 
-    grads = [g.reshape(nseq, -1, g.shape[-1]) for g in (small_grad, out_grad, gate_grad, up_grad, down_grad)]
-    small_sum, out_sum, gate_sum, up_sum, down_sum = [g.astype(F32) for g in reduce_all(near, grads)]
-    return (output, input_grad, small_sum[:, 800], small_sum[:, :96], small_sum[:, 96:480], small_sum[:, 736:768], small_sum[:, 480:608],
-            small_sum[:, 768:800], small_sum[:, 608:736], out_sum, small_sum[:, 801], gate_sum, up_sum, down_sum)
+    small_grad = small_grad.reshape(nseq, -1, 896)
+    small_sum = reduce_weights([small_grad], SMALL_UNITS, SMALL_PLAN, 3)[0] if near else reduce_far([small_grad])[0]
+    small_sum = small_sum.astype(F32)
+    out_sum, gate_sum, up_sum, down_sum = [g.astype(F32) for g in sums]
+    key_value = head_columns(small_sum[:, 736:800], 4)
+    return (output, input_grad, small_sum[:, 800], head_columns(small_sum[:, :96], QRANK), small_sum[:, 96:480], key_value[:, :32], small_sum[:, 480:608],
+            key_value[:, 32:], small_sum[:, 608:736], out_sum, small_sum[:, 801], gate_sum, up_sum, down_sum)
 
 
 def solution(mesh):

time: 587 us -> 428 us (0.73)
  Pallas kernels: 413 us -> 303 us
  local copies, waits for them, and re-layouts: 57.6 us -> 24.5 us
  other arithmetic: 30.7 us -> 22.8 us
  matrix products: 75.2 us -> 68.4 us
    pallas_call x3 -> x2, Pallas kernels: 261 us -> 150 us  [the longest x1 121 us: attend_back_reduce(): pl.pallas_call(functools.partial(back_kernel, span, min(512, nk), units,...]
    concatenate x7 -> x1, local copies, waits for them, and re-layouts: 14.4 us -> 1.12 us  [per_device(): jnp.concatenate([pair_columns(query_heads, QRANK), query_dims, key_dims,...]
    reshape x14 -> x6, local copies, waits for them, and re-layouts: 12.8 us -> 1.75 us  [the longest x4 1 us: pair_columns(): return a.reshape(-1, ranks, PAIRS, 2).transpose(0, 2, 1, 3).reshape(a.shape)]
    dot_general x16, matrix products: 75.2 us -> 68.4 us  [dot(): lax.dot_general(a, b, ((ca, cb), ((), ())), preferred_element_type=F32)]
where the time goes in v2:
time: 428 us; the launch traced here: 421 us
  Pallas kernels  303 us (71%)
  matrix products  68.4 us (16%)
  local copies, waits for them, and re-layouts  24.5 us (6%)
  other arithmetic  22.8 us (5%)
    pallas_call x1, Pallas kernels, attend_back_reduce(): pl.pallas_call(functools.partial(back_kernel, span, min(512, nk), units,...  121 us
    pallas_call x1, Pallas kernels, gather_weights(): pl.pallas_call(functools.partial(gather_kernel, specs, order), out_shape=...  92.9 us
    dot_general x16, matrix products, dot(): lax.dot_general(a, b, ((ca, cb), ((), ())), preferred_element_type=F32)  68.4 us
    pallas_call x1, Pallas kernels, gather_rows(): pl.pallas_call(gather_rows_kernel, out_shape=jax.ShapeDtypeStruct((8, *a....  32.1 us
    pallas_call x1, Pallas kernels, reduce_weights(): pl.pallas_call(functools.partial(reduce_kernel, units, narr, plan), out_s...  29.1 us
    pallas_call x1, Pallas kernels, attend(): pl.pallas_call(functools.partial(attend_kernel, span, chunk), grid=(rows,...  28.5 us

profile of v2, /device:TPU:0, one launch (start us, length us, event | category | flops | bytes accessed | tf_op | source)
XLA Modules:
  0.0 420.8 jit_solution(12756224457047147318)
XLA Ops:
  4.0 1.1 concatenate.47
  5.8 92.9 %gather_weights.1 = (bf16[8,128,896]{2,1,0:T(8,128)(2,1)}, bf16[8,128,1024]{2,1,0:T(8,128)(2,1)}, bf16[8,128,2816]{2,1,0:T(8,128)(2,1)}, bf16[8,128,2816]{2,1,0:T(8,128)(2,1)}, bf16[8,352,1024]{2,1,0:T(8,128)(2,1)}) custom-call(bf16[128,896]{1,0:T(8,128)(2,1)} %pad.4.refs_0_, bf16[128,1024]{1,0:T(8,128)(2,1)} %refs_1_.1, bf16[128,2816]{1,0:T(8,128)(2,1)} %refs_2_.1, ...), custom_call_target="tpu_custom_call" | custom-call | tf_op jit(solution)/shard_map/gather_weights/pallas_call | solution.py:147
  98.8 2.0 slice_convert_fusion
  101.6 2.3 fusion.27
  108.1 32.1 %gather_rows.1.shared_ref = bf16[8,2,320,256]{3,2,1,0:T(8,128)(2,1)} custom-call(bf16[2,320,256]{2,1,0:T(8,128)(2,1)} %pad_maximum_fusion.4.src), custom_call_target="tpu_custom_call" | custom-call | tf_op jit(solution)/shard_map/gather_rows/pallas_call | solution.py:403
  140.2 2.7 fusion.5
  150.6 28.5 %attend.1 = (bf16[2,256,1024]{2,1,0:T(8,128)(2,1)}, f32[2,256,128]{2,1,0:T(8,128)}) custom-call(f32[2,8,12,256]{3,2,1,0:T(8,128)} %copy.74.qh_ref, f32[2,384,256]{2,1,0:T(8,128)} %bitcast.161, f32[2,8,8,1024]{3,2,1,0:T(8,128)} %fusion.44.hl_ref, f32[2,8,8,1024]{3,2,1,0:T(8,128)} %fusion.43.hs_ref, bf16[2,256,1024]{2,1,0:T(8,128)(2,1)} %slice.177.dl_ref, ...), custom_call_target="tpu_custom_call" | custom-call | tf_op jit(solution)/shard_map/attend/pallas_call | solution.py:617
  179.1 2.7 multiply_reduce_fusion.2
  181.8 7.7 %fusion.56 = f32[2816,512]{0,1:T(8,128)} fusion(bf16[2816,1024]{1,0:T(8,128)(2,1)} %bitcast.220, bf16[512,1024]{1,0:T(8,128)(2,1)S(1)} %bitcast.172), kind=kOutput, calls=%fused_computation.128 | convolution fusion | flops 2952790016 | bytes 12582912 | tf_op jit(solution)/shard_map/dot_general | solution.py:963
  189.5 1.2 copy.96
  191.0 7.7 %fusion.55 = f32[512,2816]{1,0:T(8,128)} fusion(bf16[512,1024]{1,0:T(8,128)(2,1)S(1)} %multiply_convert_fusion.1, bf16[1024,2816]{1,0:T(8,128)(2,1)} %bitcast.212), kind=kOutput, calls=%fused_computation.127 | convolution fusion | flops 2952790016 | bytes 12582912 | tf_op jit(solution)/shard_map/dot_general | solution.py:963
  198.7 10.5 %fusion.4 = (bf16[512,2816]{1,0:T(8,128)(2,1)S(1)}, bf16[512,2816]{1,0:T(8,128)(2,1)}, bf16[512,2816]{1,0:T(8,128)(2,1)}) fusion(f32[2816,512]{0,1:T(8,128)} %fusion.56, f32[512,2816]{1,0:T(8,128)} %fusion.55, bf16[512,1024]{1,0:T(8,128)(2,1)S(1)} %multiply_convert_fusion.1, bf16[1024,2816]{1,0:T(8,128)(2,1)S(1)} %bitcast.218), kind=kOutput, calls=%fused_computation.6 | convolution fusion | flops 2975858688 | bytes 27000832 | tf_op jit(solution)/shard_map/dot_general | solution.py:963
  209.3 6.1 %add_convert_fusion = bf16[512,1024]{1,0:T(8,128)(2,1)} fusion(f32[512,1024]{1,0:T(8,128)S(1)} %get-tuple-element.79, bf16[512,2816]{1,0:T(8,128)(2,1)} %get-tuple-element.52, bf16[2816,1024]{1,0:T(8,128)(2,1)S(1)} %bitcast.223), kind=kOutput, calls=%fused_computation.43 | convolution fusion | flops 2953838592 | bytes 11796480 | tf_op jit(solution)/shard_map/dot_general | solution.py:963
  215.4 3.2 fusion.57
  218.6 3.4 multiply_reduce_fusion
  223.6 2.3 convolution_convert_fusion.4
  225.9 2.7 convolution_convert_fusion.3
  228.5 5.1 %convolution_convert_fusion.2 = bf16[1024,2816]{1,0:T(8,128)(2,1)} fusion(bf16[512,1024]{1,0:T(8,128)(2,1)S(1)} %multiply_convert_fusion.1, bf16[512,2816]{1,0:T(8,128)(2,1)S(1)} %copy-done.20), kind=kOutput, calls=%fused_computation.11 | convolution fusion | flops 2955673600 | bytes 9699328 | tf_op jit(solution)/shard_map/dot_general | solution.py:963
  233.6 5.0 %convolution_convert_fusion.1 = bf16[1024,2816]{1,0:T(8,128)(2,1)} fusion(bf16[512,1024]{1,0:T(8,128)(2,1)S(1)} %multiply_convert_fusion.1, bf16[512,2816]{1,0:T(8,128)(2,1)S(1)} %get-tuple-element.50), kind=kOutput, calls=%fused_computation.10 | convolution fusion | flops 2955673600 | bytes 9699328 | tf_op jit(solution)/shard_map/dot_general | solution.py:963
  238.6 5.2 %convolution_convert_fusion = bf16[2816,1024]{1,0:T(8,128)(2,1)} fusion(bf16[512,2816]{1,0:T(8,128)(2,1)S(1)} %copy-done.18, bf16[512,1024]{1,0:T(8,128)(2,1)S(1)} %bitcast.173), kind=kOutput, calls=%fused_computation.9 | convolution fusion | flops 2955673600 | bytes 9699328 | tf_op jit(solution)/shard_map/dot_general | solution.py:963
  243.8 120.8 %attend_back_reduce.1 = (f32[2,8,12,256]{3,2,1,0:T(8,128)}, f32[2,384,256]{2,1,0:T(8,128)}, bf16[2,320,256]{2,1,0:T(8,128)(2,1)}, bf16[128,1024]{1,0:T(8,128)(2,...) custom-call(f32[2,8,12,256]{3,2,1,0:T(8,128)} %copy.74.qh_ref, ...), custom_call_target="tpu_custom_call" | custom-call | tf_op jit(solution)/shard_map/attend_back_reduce/pallas_call | solution.py:919
  367.3 1.7 fusion.17
  369.0 1.9 fusion.8
  371.3 2.3 bitcast_convert_fusion
  373.6 3.0 copy.80
  376.7 1.9 maximum_maximum_fusion.refs_0_
  378.6 29.1 %reduce_weights.1 = bf16[128,896]{1,0:T(8,128)(2,1)} custom-call(bf16[8,128,896]{2,1,0:T(8,128)(2,1)} %maximum_maximum_fusion.refs_0_), custom_call_target="tpu_custom_call" | custom-call | tf_op jit(solution)/shard_map/reduce_weights/pallas_call | solution.py:353
  410.8 1.7 slice.186
  414.2 1.7 fusion.53
  416.7 1.2 convert_element_type.145
  417.9 1.2 convert_element_type.146
  419.1 1.3 convert_element_type.147
  (130 shorter events, 27.1 us)
Async XLA Ops:
  5.8 95.2 %copy-start = (bf16[2,256,1024]{2,1,0:T(8,128)(2,1)S(1)}, bf16[2,256,1024]{2,1,0:T(8,128)(2,1)}, u32[]{:S(2)}) copy-start(bf16[2,256,1024]{2,1,0:T(8,128)(2,1)} %param.16) | copy-start | bytes 3145732
  101.6 2.4 copy-start.12
  104.7 1.0 copy-start.14
  146.4 3.5 copy-start.15
  150.6 28.6 %copy-start.16 = (bf16[8,128,1024]{2,1,0:T(8,128)(2,1)S(1)}, bf16[8,128,1024]{2,1,0:T(8,128)(2,1)}, u32[]{:S(2)}) copy-start(bf16[8,128,1024]{2,1,0:T(8,128)(2,1)} %get-tuple-element.30) | copy-start | bytes 6291460
  179.1 2.7 copy-start.4
  190.7 8.0 %slice-start.2 = ((s8[5767168]{0:T(1024)(128)(4,1)}), s8[4194304]{0:T(1024)(128)(4,1)S(1)}, s32[]{:S(2)}) async-start(s8[5767168]{0:T(1024)(128)(4,1)} %bitcast.216), calls=%async_computation.2 | async-start | bytes 8388608
  191.0 7.7 %slice-start.3 = ((s8[5767168]{0:T(1024)(128)(4,1)}), s8[1572864]{0:T(1024)(128)(4,1)S(1)}, s32[]{:S(2)}) async-start(s8[5767168]{0:T(1024)(128)(4,1)} %bitcast.216), calls=%async_computation.3 | async-start | bytes 3145728
  191.0 18.2 %slice-start.4 = ((s8[5767168]{0:T(1024)(128)(4,1)}), s8[4194304]{0:T(1024)(128)(4,1)S(1)}, s32[]{:S(2)}) async-start(s8[5767168]{0:T(1024)(128)(4,1)} %bitcast.221), calls=%async_computation.4 | async-start | bytes 8388608
  198.7 10.6 %slice-start.5 = ((s8[5767168]{0:T(1024)(128)(4,1)}), s8[1572864]{0:T(1024)(128)(4,1)S(1)}, s32[]{:S(2)}) async-start(s8[5767168]{0:T(1024)(128)(4,1)} %bitcast.221), calls=%async_computation.5 | async-start | bytes 3145728
  198.7 19.8 %slice-start = ((s8[5767168]{0:T(1024)(128)(4,1)}), s8[4194304]{0:T(1024)(128)(4,1)S(1)}, s32[]{:S(2)}) async-start(s8[5767168]{0:T(1024)(128)(4,1)} %bitcast.213), calls=%async_computation | async-start | bytes 8388608
  209.3 6.1 %copy-start.19 = (bf16[512,2816]{1,0:T(8,128)(2,1)S(1)}, bf16[512,2816]{1,0:T(8,128)(2,1)}, u32[]{:S(2)}) copy-start(bf16[512,2816]{1,0:T(8,128)(2,1)} %get-tuple-element.51) | copy-start | bytes 8650756
  209.3 9.3 %slice-start.1 = ((s8[5767168]{0:T(1024)(128)(4,1)}), s8[1572864]{0:T(1024)(128)(4,1)S(1)}, s32[]{:S(2)}) async-start(s8[5767168]{0:T(1024)(128)(4,1)} %bitcast.213), calls=%async_computation.1 | async-start | bytes 3145728
  218.6 3.4 copy-start.5
  222.0 1.6 copy-start.17
  222.6 3.2 copy-start.1
  223.6 2.3 copy-start.3
  225.9 2.7 copy-start.20
  233.6 5.0 %copy-start.18 = (bf16[512,2816]{1,0:T(8,128)(2,1)S(1)}, bf16[512,2816]{1,0:T(8,128)(2,1)}, u32[]{:S(2)}) copy-start(bf16[512,2816]{1,0:T(8,128)(2,1)} %get-tuple-element.52) | copy-start | bytes 8650756
  364.6 2.2 copy-start.6
  364.6 2.4 copy-start.11
  365.6 1.6 copy-start.13
  367.3 1.7 copy-start.2
  378.6 37.2 %copy-start.10 = (bf16[128,1024]{1,0:T(8,128)(2,1)S(1)}, bf16[128,1024]{1,0:T(8,128)(2,1)}, u32[]{:S(2)}) copy-start(bf16[128,1024]{1,0:T(8,128)(2,1)} %get-tuple-element.38) | copy-start | bytes 786436
  378.6 38.1 %copy-start.9 = (bf16[128,2816]{1,0:T(8,128)(2,1)S(1)}, bf16[128,2816]{1,0:T(8,128)(2,1)}, u32[]{:S(2)}) copy-start(bf16[128,2816]{1,0:T(8,128)(2,1)} %get-tuple-element.39) | copy-start | bytes 2162692
  410.1 7.7 %copy-start.8 = (bf16[128,2816]{1,0:T(8,128)(2,1)S(1)}, bf16[128,2816]{1,0:T(8,128)(2,1)}, u32[]{:S(2)}) copy-start(bf16[128,2816]{1,0:T(8,128)(2,1)} %get-tuple-element.40) | copy-start | bytes 2162692
  416.7 2.4 copy-start.7
